TPU v7x, 32 devices: a whole 2x2x4 slice. The times are simulated.
32 devices in a mesh: seq: 4 (over z), chan: 4 (over y, x), dp: 2 (over core).
Axes of the slice: x: 2, y: 2, z: 4, core: 2. Of those that a mesh axis runs over, the one named last changes fastest.
Arguments:
- mr_query: bfloat16 [2, 8192, 512], P('dp', 'chan', 'seq'), may hold values from -6 to 6
- mr_key: bfloat16 [2, 8192, 512], P('dp', 'chan', 'seq'), may hold values from -6 to 6
- mr_value: bfloat16 [2, 8192, 512], P('dp', 'chan', 'seq'), may hold values from -6 to 6
- li_key: bfloat16 [2, 8192, 512], P('dp', 'chan', 'seq'), may hold values from -6 to 6
- li_value: bfloat16 [2, 8192, 512], P('dp', 'chan', 'seq'), may hold values from -6 to 6
- grad_out: bfloat16 [2, 8192, 512], P('dp', 'chan', 'seq'), may hold values from -6 to 6
- mr_filter: bfloat16 [512, 128], P('chan'), may hold values from -0.5 to 0.5
- li_residue: float32 [512, 16], P('chan'), may hold values from -1.5 to 1.5
- li_rate: float32 [512, 16], P('chan'), may hold values from 1.953125e-05 to 0.05
Outputs:
- grad_mr_query: bfloat16 [2, 8192, 512], P('dp', 'chan', 'seq')
- grad_mr_key: bfloat16 [2, 8192, 512], P('dp', 'chan', 'seq')
- grad_mr_value: bfloat16 [2, 8192, 512], P('dp', 'chan', 'seq')
- grad_li_key: bfloat16 [2, 8192, 512], P('dp', 'chan', 'seq')
- grad_li_value: bfloat16 [2, 8192, 512], P('dp', 'chan', 'seq')
- grad_filter: float32 [512, 128], P('chan')
- grad_residue: float32 [512, 16], P('chan')
All inputs are finite; a program needn't handle non-finite values.
Results may differ from a plain program's by a relative error of at most 0.012.
Values may be sent and summed in bfloat16 or wider, within the bound.
No kernel may reach another device: no remote copies, remote signals or barrier semaphores. Data moves between devices by JAX's collectives and lax.ppermute only.
A program may use at most 128 MiB of HBM per device.

v0:
```python
import functools

import jax
import jax.numpy as jnp
from jax import lax
from jax.experimental import pallas as pl
from jax.experimental.pallas import tpu as pltpu
from jax.sharding import PartitionSpec as P

F32 = jnp.float32
BF16 = jnp.bfloat16
TILE = 128
LANES = 16
PACK = TILE // LANES
CHUNK = 32
STEPS = 4
VMEM_LIMIT = 24 * 1024 * 1024


def nn(lhs, rhs):
    return lax.dot_general(lhs, rhs, (((1,), (0,)), ((), ())), preferred_element_type=F32)


def nt(lhs, rhs):
    return lax.dot_general(lhs, rhs, (((1,), (1,)), ((), ())), preferred_element_type=F32)


def iotas():
    rows = lax.broadcasted_iota(jnp.int32, (TILE, TILE), 0)
    cols = lax.broadcasted_iota(jnp.int32, (TILE, TILE), 1)
    return rows, cols


def ones_where(mask):
    return jnp.where(mask, 1.0, 0.0).astype(BF16)


def column(turned, mask):
    wide = jnp.concatenate([turned] * PACK, axis=0)
    return jnp.sum(jnp.where(mask, wide, 0.0), axis=1, keepdims=True)


def squeeze_groups(wide, mask):
    kept = jnp.where(mask, wide, 0.0)
    total = kept[:LANES]
    for g in range(1, PACK):
        total = total + kept[g * LANES : (g + 1) * LANES]
    return total


def spread_groups(narrow, mask):
    return jnp.where(mask, jnp.concatenate([narrow] * PACK, axis=0), 0.0)


def circulant(row):
    base = jnp.broadcast_to(row, (LANES, TILE))
    base = pltpu.roll(base, 0, 1, stride=1, stride_axis=0).astype(BF16)
    return jnp.concatenate(
        [base] + [pltpu.roll(base, LANES * j, 1) for j in range(1, PACK)], axis=0
    )


def reversal():
    rows, cols = iotas()
    return ones_where((rows + cols) % TILE == 0)


def one_minus_exp(value):
    series = jnp.full_like(value, 1.0)
    for order in (7, 6, 5, 4, 3, 2):
        series = 1.0 - value * series / order
    return jnp.where(value < 0.125, value * series, 1.0 - jnp.exp(-value))


def chunk_mask(shape, bit):
    return (lax.broadcasted_iota(jnp.int32, shape, 1) // CHUNK) & bit == 0


def pair_chunks(turned):
    parts = [turned[CHUNK * j : CHUNK * (j + 1), :] for j in range(TILE // CHUNK)]
    for bit in (1, 2):
        keep = chunk_mask((CHUNK, TILE), bit)
        for j in range(len(parts)):
            if j & bit == 0:
                low, high = parts[j], parts[j + bit]
                parts[j] = jnp.where(keep, low, pltpu.roll(high, CHUNK * bit, 1))
                parts[j + bit] = jnp.where(keep, pltpu.roll(low, TILE - CHUNK * bit, 1), high)
    return parts


def windows(before, now):
    lanes = lax.broadcasted_iota(jnp.int32, now.shape, 1)
    none = jnp.zeros_like(now)
    first, second = [none if before is None else before], [now]
    for j in range(1, TILE // CHUNK):
        left = TILE - CHUNK * j
        moved = pltpu.roll(now, left, 1)
        older = none if before is None else pltpu.roll(before, left, 1)
        first.append(jnp.where(lanes < left, older, moved))
        second.append(moved)
    return jnp.concatenate(
        [jnp.concatenate(first, axis=0), jnp.concatenate(second, axis=0)], axis=1
    )


def beside(first, second):
    return jnp.concatenate([first, second], axis=1)


def above(*arrays):
    return jnp.concatenate(arrays, axis=0)


def apart(first, second):
    none = jnp.zeros_like(first)
    return above(beside(first, none), beside(none, second))


def lag_rows(chunks, shifted_rows, own_rows):
    wide = nn(above(*[chunks * own for own in own_rows]), shifted_rows)
    rows = lax.broadcasted_iota(jnp.int32, (2 * CHUNK, TILE), 0) % CHUNK
    lanes = lax.broadcasted_iota(jnp.int32, (2 * CHUNK, TILE), 1)
    sums = jnp.where(lanes + rows < CHUNK, wide[:, TILE:], wide[:, :TILE])
    parts = []
    for start in (0, CHUNK):
        total = sums[start : start + 8]
        for turn in (8, 16, 24):
            total = total + pltpu.roll(sums[start + turn : start + turn + 8], turn, 1)
        parts.append(pltpu.roll(total, 0, 1, stride=1, stride_axis=0))
    return above(*parts).astype(BF16)


def now_and_before(now, before, rows, half):
    both = beside(now, before)
    pieces = []
    for g in range(0, PACK, 2):
        circs = beside(*[circulant(rows[h : h + 1, :]) for h in (g, g + 1)])
        w_now = circs * half
        wide = nn(both[g * LANES : (g + 2) * LANES, :], above(w_now, circs - w_now))
        pieces += [wide[:LANES, :TILE], wide[LANES:, TILE:]]
    return jnp.concatenate(pieces, axis=0)


def within_shard(array, rows, half):
    pieces = []
    for g in range(0, PACK, 4):
        weights = [
            beside(*[circulant(rows[h : h + 1, :]) for h in (k, k + 1)]) * half
            for k in (g, g + 2)
        ]
        parts = [array[k * LANES : (k + 2) * LANES, :] for k in (g, g + 2)]
        wide = nn(apart(*parts), above(*weights))
        for k in range(4):
            column_at = (k % 2) * TILE
            pieces.append(wide[k * LANES : (k + 1) * LANES, column_at : column_at + TILE])
    return jnp.concatenate(pieces, axis=0)


def block_groups(at, blocks, block):
    rows, cols = iotas()
    return cols == rows // LANES + (at * blocks + block) * PACK


def gate_kernel(query, key, product, held, made, arrived, left):
    size = held.shape[1] // STEPS

    def fetch(array, step):
        span = pl.ds(step * size, size)
        return pltpu.make_async_copy(
            (query, key)[array].at[span, :], held.at[array, span, :], arrived.at[array, step]
        )

    def store(step):
        span = pl.ds(step * size, size)
        return pltpu.make_async_copy(made.at[span, :], product.at[span, :], left.at[step])

    for step in range(STEPS):
        for array in range(2):
            fetch(array, step).start()
    for step in range(STEPS):
        for array in range(2):
            fetch(array, step).wait()
        span = pl.ds(step * size, size)
        made[span, :] = held[0, span, :] * held[1, span, :]
        store(step).start()
    for step in range(STEPS):
        store(step).wait()


def state_kernel(grad, value, rate, state):
    rows, cols = iotas()
    offsets = cols.astype(F32)
    mask = rows // LANES == cols // LANES
    at = pl.program_id(0)
    blocks = state.shape[0]
    for block in range(blocks):
        span = pl.ds(block * TILE, TILE)
        rates = column(rate[...], block_groups(at, blocks, block))
        powers = jnp.exp(-rates * offsets).astype(BF16)
        dz2 = grad[span, :] * value[span, :]
        state[block] = squeeze_groups(nt(powers, dz2), mask).astype(BF16)


def table_kernel(
    rate, residue, filters, to_next, after, to_end, power, taps, turned, mr_turned, wide_rate
):
    rows, cols = iotas()
    mask = rows // LANES == cols // LANES
    offsets = cols.astype(F32)
    lags = ((CHUNK - 1 - cols) % TILE).astype(F32)
    at = pl.program_id(0)
    blocks = power.shape[0] // TILE
    coeffs = residue[...] * jnp.sqrt(one_minus_exp(2.0 * rate[...]))
    sums = []
    for block in range(blocks):
        span = pl.ds(block * TILE, TILE)
        own = block_groups(at, blocks, block)
        rates = column(rate[...], own)
        scale = column(coeffs, own)
        wide_rate[block] = squeeze_groups(jnp.broadcast_to(rates, (TILE, TILE)), mask)
        powers = jnp.exp(-rates * offsets)
        scaled = powers * scale
        ends = jnp.exp(-rates * (TILE - 1 - offsets))
        power[span, :] = jnp.exp(-rates * lags).astype(BF16)
        to_end[span, :] = ends.astype(BF16)
        after[span, :] = scaled.astype(BF16)
        to_next[span, :] = (ends * scale).astype(BF16)
        sums.append(jnp.sum(scaled.reshape(PACK, LANES, TILE), axis=1))
    taps[...] = above(*sums)
    turned[...] = nn(above(*sums).astype(BF16), reversal())
    mr_turned[...] = nn(filters[...], reversal())


def spans(array):
    return [pl.ds(block * TILE, TILE) for block in range(array.shape[0] // TILE)]


def group_rows(table, block):
    return table[pl.ds(block * PACK, PACK), :]


def local_kernel(grad, value, turned, du2):
    rows, cols = iotas()
    lower = ones_where(rows >= cols)
    lower_half = beside(lower, lower)
    results = [
        within_shard(grad[span, :] * value[span, :], group_rows(turned, block), lower_half)
        for block, span in enumerate(spans(grad))
    ]
    for span, result in zip(spans(grad), results):
        du2[span, :] = result


def middle_kernel(states, local, to_next, li_key, value, before, dz1, du2):
    rows, cols = iotas()
    mask = rows // LANES == cols // LANES
    wides = [spread_groups(states[block], mask).T.astype(BF16) for block in range(states.shape[0])]
    totals = [
        local[span, :] + nn(wide, to_next[span, :]) for span, wide in zip(spans(local), wides)
    ]
    for span, total in zip(spans(local), totals):
        du2[span, :] = total
        dy1 = total * li_key[span, :].astype(F32)
        dz1[span, :] = (dy1 * value[span, :].astype(F32)).astype(BF16)


def forward_kernel(before, now, filters, value, li_key, to_end, z1, u2, state):
    rows, cols = iotas()
    mask = rows // LANES == cols // LANES
    upper = ones_where(cols >= rows)
    upper_half = beside(upper, upper)
    results = [
        now_and_before(
            now[span, :], before[span, :], group_rows(filters, block).astype(F32), upper_half
        )
        for block, span in enumerate(spans(now))
    ]
    halves = []
    for span, result in zip(spans(now), results):
        y1 = (value[span, :].astype(F32) * result).astype(BF16).astype(F32)
        halves.append((y1 * li_key[span, :].astype(F32)).astype(BF16))
    ends = [nt(to_end[span, :], half) for span, half in zip(spans(now), halves)]
    for block, span in enumerate(spans(now)):
        z1[span, :] = results[block]
        u2[span, :] = halves[block]
        state[block] = squeeze_groups(ends[block], mask).astype(BF16)


def sums_kernel(
    before, now, u2, dz1, grad, li_value, power, state, after_shard, rate,
    packed, filter_sums, within_sums, across_sums,
):
    rows, cols = iotas()
    turn = ones_where(cols == rows - rows % CHUNK + (CHUNK - 1 - rows % CHUNK))
    lanes = lax.broadcasted_iota(jnp.int32, (CHUNK, TILE), 1)
    own_rows = [ones_where((lanes // LANES) % 2 == i) for i in range(2)]
    at = pl.program_id(0)
    blocks = now.shape[0] // TILE

    @pl.when(at == 0)
    def _():
        within_sums[...] = jnp.zeros_like(within_sums)
        across_sums[...] = jnp.zeros_like(across_sums)

    eights = ones_where(
        lax.broadcasted_iota(jnp.int32, (2 * PACK, TILE), 1) // 8
        == lax.broadcasted_iota(jnp.int32, (2 * PACK, TILE), 0)
    )
    turned = []
    for span in spans(now):
        dz2 = grad[span, :] * li_value[span, :]
        turned.append(nt(turn, above(dz1[span, :], dz2)).astype(BF16))
    chunks = [(pair_chunks(each[:, :TILE]), pair_chunks(each[:, TILE:])) for each in turned]
    lags, energies = [], []
    for block in range(blocks):
        lag, energy = [], []
        for p in range(TILE // CHUNK):
            pair = pl.ds(block * TILE + p * CHUNK, CHUNK)
            older, newer = before[pair, :], now[pair, :]
            lag.append(lag_rows(chunks[block][0][p], windows(older, newer), own_rows))
            energy.append(lag_rows(chunks[block][1][p], windows(None, u2[pair, :]), own_rows))
        both = nn(eights, above(*lag, *energy))
        lags.append(both[:PACK])
        energies.append(above(*[both[PACK:].astype(BF16)] * LANES))
    within, across = jnp.zeros((LANES, TILE), F32), jnp.zeros((LANES, TILE), F32)
    for block, span in enumerate(spans(now)):
        own = block_groups(at, blocks, block)
        within = within + squeeze_groups(nt(power[span, :], energies[block]), own)
        crossing = state[block].astype(F32) * after_shard[block]
        across = across + nn(crossing.astype(BF16), ones_where(own))
        packed[at * blocks + block] = state[block]
    few = blocks * PACK
    filter_sums[pl.ds(pl.multiple_of(at * few, few), few), :] = above(*lags)
    within_sums[...] += within
    across_sums[...] += across

    steps = filter_sums.shape[0] // few

    @pl.when(at == steps - 1)
    def _():
        place = ones_where((rows + cols) % TILE == CHUNK - 1)
        sums = nn(filter_sums[...].astype(BF16), place).astype(BF16)
        for chunk in range(filter_sums.shape[0] // LANES):
            packed[steps * blocks + chunk] = sums[chunk * LANES : (chunk + 1) * LANES]
        gains = jnp.sqrt(one_minus_exp(2.0 * rate[...]))
        total = gains * (within_sums[...] + across_sums[...])
        packed[steps * blocks + filter_sums.shape[0] // LANES] = total.astype(BF16)


def within_kernel(
    bits, u2, taps, wide_rate, z1, du2, value, li_key, later,
    z2, grad_value, grad_key, zeros, *weights,
):
    zeros[...] = jnp.zeros_like(zeros)
    place = lax.axis_index("seq")
    rates = wide_rate[...]
    weights = list(weights)
    for bit in bits:
        high = (place & bit) != 0
        passed = TILE * (place & (bit - 1)) + 1
        reach = jnp.exp(-rates * passed.astype(F32))
        weights.pop(0)[...] = jnp.where(high, reach, 0.0)
        if bit != bits[-1]:
            run = jnp.exp(-rates * (TILE * bit))
            one = jnp.ones_like(run)
            weights.pop(0)[...] = jnp.where(high, run, one)
            weights.pop(0)[...] = jnp.where(high, one, run)
    rows, cols = iotas()
    upper = ones_where(cols >= rows)
    upper_half = beside(upper, upper)
    results = [
        within_shard(u2[span, :], group_rows(taps, block), upper_half)
        for block, span in enumerate(spans(u2))
    ]
    for span, result in zip(spans(u2), results):
        z2[span, :] = result
        z1_here, du2_here = z1[span, :], du2[span, :]
        y1 = (value[span, :].astype(F32) * z1_here).astype(BF16).astype(F32)
        grad_key[span, :] = (du2_here * y1).astype(BF16)
        grad_value[span, :] = (du2_here * li_key[span, :].astype(F32) * z1_here).astype(BF16)


def last_kernel(half, other, grad_filter, grad_residue):
    chunks = half.shape[0] - 1
    for chunk in range(chunks):
        grad_filter[pl.ds(chunk * LANES, LANES), :] = half[chunk].astype(F32) + other[chunk].astype(F32)
    grad_residue[...] = half[chunks].astype(F32) + other[chunks].astype(F32)


def product_kernel(dz1, later, turned, query, key, grad_query, grad_key, nothing):
    nothing[...] = jnp.zeros_like(nothing)
    rows, cols = iotas()
    lower = ones_where(rows >= cols)
    lower_half = beside(lower, lower)
    results = [
        now_and_before(
            dz1[span, :], later[span, :], group_rows(turned, block), lower_half
        )
        for block, span in enumerate(spans(dz1))
    ]
    for span, du1 in zip(spans(dz1), results):
        grad_query[span, :] = (du1 * key[span, :].astype(F32)).astype(BF16)
        grad_key[span, :] = (du1 * query[span, :].astype(F32)).astype(BF16)


def value_kernel(states, after, z2, grad, grad_value):
    rows, cols = iotas()
    mask = rows // LANES == cols // LANES
    wides = [spread_groups(states[block], mask).T.astype(BF16) for block in range(states.shape[0])]
    totals = [z2[span, :] + nn(wide, after[span, :]) for span, wide in zip(spans(z2), wides)]
    for span, total in zip(spans(z2), totals):
        grad_value[span, :] = (grad[span, :].astype(F32) * total).astype(BF16)


def shifted(value, axis, steps):
    count = lax.axis_size(axis)
    first, last = max(0, -steps), min(count, count - steps)
    return lax.ppermute(value, axis, [(source, source + steps) for source in range(first, last)])


def swapped(value, axis, bit):
    count = lax.axis_size(axis)
    return lax.ppermute(value, axis, [(source, source ^ bit) for source in range(count)])


def scan_bits():
    count, bit, bits = lax.axis_size("seq"), 1, []
    assert count & (count - 1) == 0
    while bit < count:
        bits.append(bit)
        bit *= 2
    return bits


def per_device(
    mr_query, mr_key, mr_value, li_key, li_value, grad_out, mr_filter, li_residue, li_rate
):
    query, key, value, key_two, value_two, grad = (
        array[0] for array in (mr_query, mr_key, mr_value, li_key, li_value, grad_out)
    )
    groups, filt_len = mr_filter.shape
    channels, seq_local = query.shape
    assert filt_len == TILE and seq_local == TILE and groups <= TILE
    assert channels == groups * LANES and li_rate.shape[1] == LANES
    rows = channels // STEPS
    few = groups // STEPS
    spare = ((0, 0), (0, TILE - groups))
    rate = jnp.pad(li_rate.T, spare)
    residue = jnp.pad(li_residue.T, spare)

    blocks = channels // TILE

    wide = pl.BlockSpec((rows, TILE), lambda i: (i, 0))
    table = pl.BlockSpec((few, TILE), lambda i: (i, 0))
    chunk = pl.BlockSpec((blocks // STEPS, LANES, TILE), lambda i: (i, 0, 0))
    modes = pl.BlockSpec((LANES, TILE), lambda i: (0, 0))
    distant = pl.BlockSpec(memory_space=pltpu.HBM)
    anywhere = pl.BlockSpec(memory_space=pl.ANY)
    wide_half = jax.ShapeDtypeStruct((channels, TILE), BF16)
    wide_full = jax.ShapeDtypeStruct((channels, TILE), F32)
    table_full = jax.ShapeDtypeStruct((groups, TILE), F32)
    chunk_half = jax.ShapeDtypeStruct((blocks, LANES, TILE), BF16)
    chunk_full = jax.ShapeDtypeStruct((blocks, LANES, TILE), F32)

    def call(kernel, name, in_specs, out_specs, out_shape, scratch=(), grid=STEPS, limit=VMEM_LIMIT, work=0):
        return pl.pallas_call(
            kernel,
            grid=(grid,),
            in_specs=in_specs,
            out_specs=out_specs,
            out_shape=out_shape,
            scratch_shapes=scratch,
            name=name,
            cost_estimate=pl.CostEstimate(
                flops=2 * work * channels * TILE * TILE, bytes_accessed=1, transcendentals=0
            ),
            compiler_params=pltpu.CompilerParams(vmem_limit_bytes=limit),
        )

    def whole(leaf):
        return pl.BlockSpec(leaf.shape, lambda i: (0,) * len(leaf.shape))

    def twice(spec):
        return pl.BlockSpec((2 * spec.block_shape[0],) + spec.block_shape[1:], spec.index_map)

    (product,) = call(
        gate_kernel, "gate", [distant] * 2, [distant], [wide_half],
        [
            pltpu.VMEM((2, channels, TILE), BF16), pltpu.VMEM((channels, TILE), BF16),
            pltpu.SemaphoreType.DMA((2, STEPS)), pltpu.SemaphoreType.DMA((STEPS,)),
        ],
        grid=1, limit=60 * 1024 * 1024,
    )(query, key)
    product_before = shifted(product, "seq", 1)

    (back,) = call(state_kernel, "state", [wide, wide, modes], [chunk], [chunk_half])(
        grad, value_two, rate
    )

    later_backs = [shifted(back, "seq", -gap) for gap in range(1, lax.axis_size("seq"))]
    to_next, after, to_end, power, taps, turned, mr_turned, wide_rate = call(
        table_kernel, "table", [modes, modes, table], [wide] * 4 + [table] * 3 + [chunk],
        [wide_half] * 4 + [table_full] * 3 + [chunk_full],
    )(rate, residue, mr_filter)
    fade = jnp.exp(-TILE * wide_rate)
    after_shard = later_backs[-1].astype(F32)
    for other in later_backs[-2::-1]:
        after_shard = other.astype(F32) + fade * after_shard
    after_shard = after_shard * jnp.exp(-wide_rate)

    (du2_local,) = call(
        local_kernel, "local", [wide, wide, table], [wide], [wide_full]
    )(
        grad, value_two, turned
    )

    dz1, du2 = call(
        middle_kernel, "middle", [chunk, wide, wide, wide, wide, anywhere], [wide, wide],
        [wide_half, wide_full],
    )(after_shard, du2_local, to_next, key_two, value, product_before)
    dz1_later = shifted(dz1, "seq", -1)

    z1, u2, state = call(
        forward_kernel, "forward",
        [wide, wide, table, wide, wide, wide],
        [wide, wide, chunk], [wide_full, wide_half, chunk_half],
    )(product_before, product, mr_filter, value, key_two, to_end)

    filter_chunks = groups // LANES
    packed_shape = jax.ShapeDtypeStruct((blocks + filter_chunks + 1, LANES, TILE), BF16)
    (packed,) = call(
        sums_kernel, "sums",
        [twice(wide)] * 7 + [twice(chunk), twice(chunk), modes],
        [whole(packed_shape)], [packed_shape],
        [pltpu.VMEM((groups, TILE), F32)] + [pltpu.VMEM((LANES, TILE), F32)] * 2,
        grid=STEPS // 2,
    )(product_before, product, u2, dz1, grad, value_two, power, state, after_shard, rate)

    bits = scan_bits()
    few_full = jax.ShapeDtypeStruct((filter_chunks + 1, LANES, TILE), F32)
    factors = 3 * len(bits) - 2
    z2, grad_mr_value, grad_li_key, within_zeros, *weights = call(
        functools.partial(within_kernel, bits), "within",
        [wide, table, chunk, wide, wide, wide, wide, anywhere],
        [wide, wide, wide, whole(few_full)] + [chunk] * factors,
        [wide_full, wide_half, wide_half, few_full] + [chunk_full] * factors,
    )(u2, taps, wide_rate, z1, du2, value, key_two, dz1_later)

    grad_query, grad_key, product_zeros = call(
        product_kernel, "product",
        [wide, wide, table, wide, wide], [wide, wide, whole(few_full)],
        [wide_half, wide_half, few_full],
    )(dz1, dz1_later, mr_turned, query, key)

    zeros = [within_zeros, product_zeros]
    before_shard = jnp.zeros(back.shape, F32)
    for bit in bits:
        other = swapped(packed, "seq", bit)
        sums = packed[blocks:].astype(F32) + other[blocks:].astype(F32)
        if zeros:
            sums = sums + zeros.pop(0)
        mine, theirs = packed[:blocks].astype(F32), other[:blocks].astype(F32)
        before_shard = before_shard + weights.pop(0) * theirs
        if bit != bits[-1]:
            total = weights.pop(0) * theirs + weights.pop(0) * mine
            packed = jnp.concatenate([total.astype(BF16), sums.astype(BF16)], axis=0)
    sums = sums.astype(BF16)

    assert lax.axis_size("dp") == 2
    partner = swapped(sums, "dp", 1)
    (grad_li_value,) = call(
        value_kernel, "value", [chunk, wide, wide, wide], [wide], [wide_half]
    )(before_shard, after, z2, grad)

    residue_full = jax.ShapeDtypeStruct((LANES, TILE), F32)
    grad_filter, grad_residue = call(
        last_kernel, "last", [whole(sums)] * 2,
        [whole(table_full), whole(residue_full)], [table_full, residue_full], grid=1,
    )(sums, partner)
    return (
        grad_query[None],
        grad_key[None],
        grad_mr_value[None],
        grad_li_key[None],
        grad_li_value[None],
        grad_filter,
        grad_residue[:, :groups].T,
    )


def solution(mesh):
    streams = (P("dp", "chan", "seq"),)
    tables = (P("chan", None),)
    return jax.shard_map(
        per_device,
        mesh=mesh,
        in_specs=streams * 6 + tables * 3,
        out_specs=streams * 5 + tables * 2,
        check_vma=False,
    )
```

profile of v0, /device:TPU:0, one launch (start us, length us, event | category | flops | bytes accessed | tf_op | source)
XLA Modules:
  0.0 50.6 jit_solution(9470143997453907405)
XLA Ops:
  0.6 0.0 copy-start
  0.6 0.0 copy-start.4
  0.7 0.0 copy-start.8
  0.7 2.1 %gate.1.now = bf16[2048,128]{1,0:T(8,128)(2,1)} custom-call(bf16[2048,128]{1,0:T(8,128)(2,1)} %bitcast.27, bf16[2048,128]{1,0:T(8,128)(2,1)} %bitcast.29), custom_call_target="tpu_custom_call" | custom-call | bytes 1 | tf_op jit(solution)/shard_map/gate/pallas_call | solution.py:486
  2.8 5.0 %collective-permute-start.3 = (bf16[2048,128]{1,0:T(8,128)(2,1)}, bf16[2048,128]{1,0:T(8,128)(2,1)S(1)}, u32[]{:S(2)}, u32[]{:S(2)}) collective-permute-start(bf16[2048,128]{1,0:T(8,128)(2,1)} %gate.1.now), channel_id=1, source_target_pairs={{0,8},{8,16},{16,24},{1,9},{9,17},{17,25},{2,10},{10,18},{18,26},{... | collective-permute-start | bytes 1572872 | tf_op jit(solution)/shard_map/ppermute | solution.py:418
  7.8 0.0 copy-done
  7.8 0.0 copy-done.4
  7.8 0.0 copy-done.8
  7.8 0.0 copy-start.7
  7.8 0.0 copy-start.9
  7.8 1.2 %state.1 = bf16[16,16,128]{2,1,0:T(8,128)(2,1)S(1)} custom-call(bf16[2048,128]{1,0:T(8,128)(2,1)S(1)} %bitcast.14, bf16[2048,128]{1,0:T(8,128)(2,1)S(1)} %bitcast.24, f32[16,128]{1,0:T(8,128)S(1)} %bitcast.31), custom_call_target="tpu_custom_call" | custom-call | bytes 1 | tf_op jit(solution)/shard_map/state/pallas_call | solution.py:496
  9.0 1.3 %collective-permute-start = (bf16[16,16,128]{2,1,0:T(8,128)(2,1)S(1)}, bf16[16,16,128]{2,1,0:T(8,128)(2,1)S(1)}, u32[]{:S(2)}, u32[]{:S(2)}) collective-permute-start(bf16[16,16,128]{2,1,0:T(8,128)(2,1)S(1)} %state.1), channel_id=1, source_target_pairs={{8,0},{16,8},{24,16},{9,1},{17,9},{25,17},{10,2},{18,10},{26,18},{... | collective-permute-start | bytes 196616 | tf_op jit(solution)/shard_map/ppermute | solution.py:418
  10.3 1.3 %collective-permute-start.1 = (bf16[16,16,128]{2,1,0:T(8,128)(2,1)S(1)}, bf16[16,16,128]{2,1,0:T(8,128)(2,1)S(1)}, u32[]{:S(2)}, u32[]{:S(2)}) collective-permute-start(bf16[16,16,128]{2,1,0:T(8,128)(2,1)S(1)} %state.1), channel_id=1, source_target_pairs={{16,0},{24,8},{17,1},{25,9},{18,2},{26,10},{19,3},{27,11},{20,4},{... | collective-permute-start | bytes 196616 | tf_op jit(solution)/shard_map/ppermute | solution.py:418
  11.6 1.3 %collective-permute-start.2 = (bf16[16,16,128]{2,1,0:T(8,128)(2,1)S(1)}, bf16[16,16,128]{2,1,0:T(8,128)(2,1)S(1)}, u32[]{:S(2)}, u32[]{:S(2)}) collective-permute-start(bf16[16,16,128]{2,1,0:T(8,128)(2,1)S(1)} %state.1), channel_id=1, source_target_pairs={{24,0},{25,1},{26,2},{27,3},{28,4},{29,5},{30,6},{31,7}} | collective-permute-start | bytes 196616 | tf_op jit(solution)/shard_map/ppermute | solution.py:418
  12.9 0.0 copy-done.7
  12.9 0.0 copy-done.9
  12.9 1.6 %table.1 = (bf16[2048,128]{1,0:T(8,128)(2,1)S(1)}, bf16[2048,128]{1,0:T(8,128)(2,1)S(1)}, bf16[2048,128]{1,0:T(8,128)(2,1)S(1)}, bf16[2048,128]{1,0:T(8,128)(2,1...) custom-call(f32[16,128]{1,0:T(8,128)S(1)} %bitcast.32, ...), custom_call_target="tpu_custom_call" | custom-call | bytes 1 | tf_op jit(solution)/shard_map/table/pallas_call | solution.py:501
  14.5 0.0 copy-start.1
  14.5 0.0 copy-start.2
  14.5 2.3 %local.1 = f32[2048,128]{1,0:T(8,128)S(1)} custom-call(bf16[2048,128]{1,0:T(8,128)(2,1)S(1)} %bitcast.15, bf16[2048,128]{1,0:T(8,128)(2,1)S(1)} %bitcast.25, f32[128,128]{1,0:T(8,128)S(1)} %get-tuple-element.34.turned), custom_call_target="tpu_custom_call" | custom-call | bytes 1 | tf_op jit(solution)/shard_map/local/pallas_call | solution.py:511
  16.8 0.0 collective-permute-done
  16.8 1.4 %collective-permute-done.1 = bf16[16,16,128]{2,1,0:T(8,128)(2,1)S(1)} collective-permute-done((bf16[16,16,128]{2,1,0:T(8,128)(2,1)S(1)}, bf16[16,16,128]{2,1,0:T(8,128)(2,1)S(1)}, u32[]{:S(2)}, u32[]{:S(2)}) %collective-permute-start.1) | collective-permute-done | bytes 65568 | tf_op jit(solution)/shard_map/ppermute | solution.py:418
  18.2 2.6 %collective-permute-done.2 = bf16[16,16,128]{2,1,0:T(8,128)(2,1)S(1)} collective-permute-done((bf16[16,16,128]{2,1,0:T(8,128)(2,1)S(1)}, bf16[16,16,128]{2,1,0:T(8,128)(2,1)S(1)}, u32[]{:S(2)}, u32[]{:S(2)}) %collective-permute-start.2) | collective-permute-done | bytes 65568 | tf_op jit(solution)/shard_map/ppermute | solution.py:418
  20.7 0.1 exponential_multiply_fusion.states.after_shard
  20.8 0.0 collective-permute-done.3.before
  20.8 0.0 copy-done.1
  20.8 0.0 copy-done.2
  20.8 0.0 copy-start.3
  20.9 1.1 %middle.1 = (bf16[2048,128]{1,0:T(8,128)(2,1)S(1)}, f32[2048,128]{1,0:T(8,128)S(1)}) custom-call(f32[16,16,128]{2,1,0:T(8,128)S(1)} %exponential_multiply_fusion.states.after_shard, f32[2048,128]{1,0:T(8,128)S(1)} %local.1, bf16[2048,128]{1,0:T(8,128)(2,1)S(1)} %get-tuple-element.35.to_next, bf16[2048,128]{1,0:T(8,128)(2,1)S(1)} %bitcast.18, ...), custom_call_target="tpu_custom_call" | custom-call | bytes 1 | tf_op jit(solution)/shard_map/middle/pallas_call | solution.py:517
  22.0 1.3 %collective-permute-start.4 = (bf16[2048,128]{1,0:T(8,128)(2,1)S(1)}, bf16[2048,128]{1,0:T(8,128)(2,1)S(1)}, u32[]{:S(2)}, u32[]{:S(2)}) collective-permute-start(bf16[2048,128]{1,0:T(8,128)(2,1)S(1)} %get-tuple-element.36.dz1), channel_id=1, source_target_pairs={{8,0},{16,8},{24,16},{9,1},{17,9},{25,17},{10,2},{18,10},{26,18},{... | collective-permute-start | bytes 1572872 | tf_op jit(solution)/shard_map/ppermute | solution.py:418
  23.3 0.0 copy-done.3
  23.3 3.4 %forward.1 = (f32[2048,128]{1,0:T(8,128)S(1)}, bf16[2048,128]{1,0:T(8,128)(2,1)S(1)}, bf16[16,16,128]{2,1,0:T(8,128)(2,1)S(1)}) custom-call(bf16[2048,128]{1,0:T(8,128)(2,1)S(1)} %collective-permute-done.3.before, bf16[2048,128]{1,0:T(8,128)(2,1)S(1)} %copy-done.3, bf16[128,128]{1,0:T(8,128)(2,1)S(1)} %copy-done.7, bf16[2048,128]{1,0:T(8,128)(2,1)S(1)} %bitcast.22, ...), custom_call_target="tpu_custom_call" | custom-call | bytes 1 | tf_op jit(solution)/shard_map/forward/pallas_call | solution.py:523
  26.7 8.5 %sums.1 = bf16[25,16,128]{2,1,0:T(8,128)(2,1)S(1)} custom-call(bf16[2048,128]{1,0:T(8,128)(2,1)S(1)} %collective-permute-done.3.before, bf16[2048,128]{1,0:T(8,128)(2,1)S(1)} %copy-done.3, bf16[2048,128]{1,0:T(8,128)(2,1)S(1)} %get-tuple-element.41.u2, bf16[2048,128]{1,0:T(8,128)(2,1)S(1)} %get-tuple-element.36.dz1, bf16[2048,128]{1,0:T(8,128)(2,1)S(1)} %bitcast.16, ...), custom_call_target="tpu_custom_call" | custom-call | bytes 1 | tf_op jit(solution)/shard_map/sums/pallas_call | solution.py:531
  35.1 2.7 %collective-permute-start.5 = (bf16[25,16,128]{2,1,0:T(8,128)(2,1)S(1)}, bf16[25,16,128]{2,1,0:T(8,128)(2,1)S(1)}, u32[]{:S(2)}, u32[]{:S(2)}) collective-permute-start(bf16[25,16,128]{2,1,0:T(8,128)(2,1)S(1)} %sums.1), channel_id=1, source_target_pairs={{0,8},{8,0},{16,24},{24,16},{1,9},{9,1},{17,25},{25,17},{2,10},{10... | collective-permute-start | bytes 307208 | tf_op jit(solution)/shard_map/ppermute | solution.py:423
  37.8 0.0 collective-permute-done.4.later
  37.8 0.0 copy-start.6
  37.8 3.1 %within.1 = (f32[2048,128]{1,0:T(8,128)S(1)}, bf16[2048,128]{1,0:T(8,128)(2,1)}, bf16[2048,128]{1,0:T(8,128)(2,1)}, f32[9,16,128]{2,1,0:T(8,128)S(1)}, f32[16,16...) custom-call(bf16[2048,128]{1,0:T(8,128)(2,1)S(1)} %get-tuple-element.41, ...), custom_call_target="tpu_custom_call" | custom-call | bytes 1 | tf_op jit(solution)/shard_map/within/pallas_call | solution.py:542
  40.9 0.0 copy-start.5
  40.9 0.0 collective-permute-done.5
  41.0 1.9 %collective-permute-start.6 = (bf16[25,16,128]{2,1,0:T(8,128)(2,1)S(1)}, bf16[25,16,128]{2,1,0:T(8,128)(2,1)S(1)}, u32[]{:S(2)}, u32[]{:S(2)}) collective-permute-start(bf16[25,16,128]{2,1,0:T(8,128)(2,1)S(1)} %pad_maximum_fusion), channel_id=1, source_target_pairs={{0,16},{8,24},{16,0},{24,8},{1,17},{9,25},{17,1},{25,9},{2,18},{10... | collective-permute-start | bytes 307208 | tf_op jit(solution)/shard_map/ppermute | solution.py:423
  42.9 0.0 copy-done.6
  42.9 0.0 copy-done.5
  42.9 3.7 %product.1 = (bf16[2048,128]{1,0:T(8,128)(2,1)}, bf16[2048,128]{1,0:T(8,128)(2,1)}, f32[9,16,128]{2,1,0:T(8,128)S(1)}) custom-call(bf16[2048,128]{1,0:T(8,128)(2,1)S(1)} %get-tuple-element.36.dz1, bf16[2048,128]{1,0:T(8,128)(2,1)S(1)} %collective-permute-done.4.later, f32[128,128]{1,0:T(8,128)S(1)} %get-tuple-element.37.turned, ...), custom_call_target="tpu_custom_call" | custom-call | bytes 1 | tf_op jit(solution)/shard_map/product/pallas_call | solution.py:549
  46.6 1.2 %collective-permute-done.6 = bf16[25,16,128]{2,1,0:T(8,128)(2,1)S(1)} collective-permute-done((bf16[25,16,128]{2,1,0:T(8,128)(2,1)S(1)}, bf16[25,16,128]{2,1,0:T(8,128)(2,1)S(1)}, u32[]{:S(2)}, u32[]{:S(2)}) %collective-permute-start.6) | collective-permute-done | bytes 102432 | tf_op jit(solution)/shard_map/ppermute | solution.py:423
  47.8 0.1 collective-permute-start.7
  47.9 2.1 %value.1 = bf16[2048,128]{1,0:T(8,128)(2,1)} custom-call(f32[16,16,128]{2,1,0:T(8,128)S(1)} %fusion.states, bf16[2048,128]{1,0:T(8,128)(2,1)S(1)} %get-tuple-element.54.after, f32[2048,128]{1,0:T(8,128)S(1)} %get-tuple-element.55.z2, bf16[2048,128]{1,0:T(8,128)(2,1)S(1)} %bitcast.17), custom_call_target="tpu_custom_call" | custom-call | bytes 1 | tf_op jit(solution)/shard_map/value/pallas_call | solution.py:571
  50.0 0.0 collective-permute-done.7.other
  50.0 0.6 %last.1 = (f32[128,128]{1,0:T(8,128)}, f32[16,128]{1,0:T(8,128)}) custom-call(bf16[9,16,128]{2,1,0:T(8,128)(2,1)S(1)} %add_convert_fusion.half, bf16[9,16,128]{2,1,0:T(8,128)(2,1)S(1)} %collective-permute-done.7.other), custom_call_target="tpu_custom_call" | custom-call | bytes 1 | tf_op jit(solution)/shard_map/last/pallas_call | solution.py:576
  (5 shorter events, 0.1 us)
Async XLA Ops:
  0.6 7.2 %copy-start = (bf16[1,2048,128]{2,1,0:T(8,128)(2,1)S(1)}, bf16[1,2048,128]{2,1,0:T(8,128)(2,1)}, u32[]{:S(2)}) copy-start(bf16[1,2048,128]{2,1,0:T(8,128)(2,1)} %param.14) | copy-start | bytes 1572868
  0.6 7.2 %copy-start.4 = (bf16[1,2048,128]{2,1,0:T(8,128)(2,1)S(1)}, bf16[1,2048,128]{2,1,0:T(8,128)(2,1)}, u32[]{:S(2)}) copy-start(bf16[1,2048,128]{2,1,0:T(8,128)(2,1)} %param.13) | copy-start | bytes 1572868
  0.7 7.2 %copy-start.8 = (f32[128,16]{0,1:T(8,128)S(1)}, f32[128,16]{0,1:T(8,128)}, u32[]{:S(2)}) copy-start(f32[128,16]{0,1:T(8,128)} %param.17) | copy-start | bytes 24580
  2.8 18.0 %collective-permute-start.3 = (bf16[2048,128]{1,0:T(8,128)(2,1)}, bf16[2048,128]{1,0:T(8,128)(2,1)S(1)}, u32[]{:S(2)}, u32[]{:S(2)}) collective-permute-start(bf16[2048,128]{1,0:T(8,128)(2,1)} %gate.1.now), channel_id=1, source_target_pairs={{0,8},{8,16},{16,24},{1,9},{9,17},{17,25},{2,10},{10,18},{18,26},{... | collective-permute-start | bytes 1572872 | tf_op jit(solution)/shard_map/ppermute | solution.py:418
  7.8 5.1 %copy-start.7 = (bf16[128,128]{1,0:T(8,128)(2,1)S(1)}, bf16[128,128]{1,0:T(8,128)(2,1)}, u32[]{:S(2)}) copy-start(bf16[128,128]{1,0:T(8,128)(2,1)} %filters.3) | copy-start | bytes 98308
  7.8 5.1 %copy-start.9 = (f32[128,16]{0,1:T(8,128)S(1)}, f32[128,16]{0,1:T(8,128)}, u32[]{:S(2)}) copy-start(f32[128,16]{0,1:T(8,128)} %param.16) | copy-start | bytes 24580
  9.0 7.8 %collective-permute-start = (bf16[16,16,128]{2,1,0:T(8,128)(2,1)S(1)}, bf16[16,16,128]{2,1,0:T(8,128)(2,1)S(1)}, u32[]{:S(2)}, u32[]{:S(2)}) collective-permute-start(bf16[16,16,128]{2,1,0:T(8,128)(2,1)S(1)} %state.1), channel_id=1, source_target_pairs={{8,0},{16,8},{24,16},{9,1},{17,9},{25,17},{10,2},{18,10},{26,18},{... | collective-permute-start | bytes 196616 | tf_op jit(solution)/shard_map/ppermute | solution.py:418
  10.3 7.8 %collective-permute-start.1 = (bf16[16,16,128]{2,1,0:T(8,128)(2,1)S(1)}, bf16[16,16,128]{2,1,0:T(8,128)(2,1)S(1)}, u32[]{:S(2)}, u32[]{:S(2)}) collective-permute-start(bf16[16,16,128]{2,1,0:T(8,128)(2,1)S(1)} %state.1), channel_id=1, source_target_pairs={{16,0},{24,8},{17,1},{25,9},{18,2},{26,10},{19,3},{27,11},{20,4},{... | collective-permute-start | bytes 196616 | tf_op jit(solution)/shard_map/ppermute | solution.py:418
  11.6 9.1 %collective-permute-start.2 = (bf16[16,16,128]{2,1,0:T(8,128)(2,1)S(1)}, bf16[16,16,128]{2,1,0:T(8,128)(2,1)S(1)}, u32[]{:S(2)}, u32[]{:S(2)}) collective-permute-start(bf16[16,16,128]{2,1,0:T(8,128)(2,1)S(1)} %state.1), channel_id=1, source_target_pairs={{24,0},{25,1},{26,2},{27,3},{28,4},{29,5},{30,6},{31,7}} | collective-permute-start | bytes 196616 | tf_op jit(solution)/shard_map/ppermute | solution.py:418
  14.5 6.3 %copy-start.1 = (bf16[1,2048,128]{2,1,0:T(8,128)(2,1)S(1)}, bf16[1,2048,128]{2,1,0:T(8,128)(2,1)}, u32[]{:S(2)}) copy-start(bf16[1,2048,128]{2,1,0:T(8,128)(2,1)} %param.12) | copy-start | bytes 1572868
  14.5 6.3 %copy-start.2 = (bf16[1,2048,128]{2,1,0:T(8,128)(2,1)S(1)}, bf16[1,2048,128]{2,1,0:T(8,128)(2,1)}, u32[]{:S(2)}) copy-start(bf16[1,2048,128]{2,1,0:T(8,128)(2,1)} %param.11) | copy-start | bytes 1572868
  20.8 2.4 %copy-start.3 = (bf16[2048,128]{1,0:T(8,128)(2,1)S(1)}, bf16[2048,128]{1,0:T(8,128)(2,1)}, u32[]{:S(2)}) copy-start(bf16[2048,128]{1,0:T(8,128)(2,1)} %gate.1.now) | copy-start | bytes 1572868
  22.0 15.9 %collective-permute-start.4 = (bf16[2048,128]{1,0:T(8,128)(2,1)S(1)}, bf16[2048,128]{1,0:T(8,128)(2,1)S(1)}, u32[]{:S(2)}, u32[]{:S(2)}) collective-permute-start(bf16[2048,128]{1,0:T(8,128)(2,1)S(1)} %get-tuple-element.36.dz1), channel_id=1, source_target_pairs={{8,0},{16,8},{24,16},{9,1},{17,9},{25,17},{10,2},{18,10},{26,18},{... | collective-permute-start | bytes 1572872 | tf_op jit(solution)/shard_map/ppermute | solution.py:418
  35.1 5.8 %collective-permute-start.5 = (bf16[25,16,128]{2,1,0:T(8,128)(2,1)S(1)}, bf16[25,16,128]{2,1,0:T(8,128)(2,1)S(1)}, u32[]{:S(2)}, u32[]{:S(2)}) collective-permute-start(bf16[25,16,128]{2,1,0:T(8,128)(2,1)S(1)} %sums.1), channel_id=1, source_target_pairs={{0,8},{8,0},{16,24},{24,16},{1,9},{9,1},{17,25},{25,17},{2,10},{10... | collective-permute-start | bytes 307208 | tf_op jit(solution)/shard_map/ppermute | solution.py:423
  37.8 5.1 %copy-start.6 = (bf16[1,2048,128]{2,1,0:T(8,128)(2,1)S(1)}, bf16[1,2048,128]{2,1,0:T(8,128)(2,1)}, u32[]{:S(2)}) copy-start(bf16[1,2048,128]{2,1,0:T(8,128)(2,1)} %param.10) | copy-start | bytes 1572868
  40.9 2.0 %copy-start.5 = (bf16[1,2048,128]{2,1,0:T(8,128)(2,1)S(1)}, bf16[1,2048,128]{2,1,0:T(8,128)(2,1)}, u32[]{:S(2)}) copy-start(bf16[1,2048,128]{2,1,0:T(8,128)(2,1)} %param.9) | copy-start | bytes 1572868
  41.0 6.7 %collective-permute-start.6 = (bf16[25,16,128]{2,1,0:T(8,128)(2,1)S(1)}, bf16[25,16,128]{2,1,0:T(8,128)(2,1)S(1)}, u32[]{:S(2)}, u32[]{:S(2)}) collective-permute-start(bf16[25,16,128]{2,1,0:T(8,128)(2,1)S(1)} %pad_maximum_fusion), channel_id=1, source_target_pairs={{0,16},{8,24},{16,0},{24,8},{1,17},{9,25},{17,1},{25,9},{2,18},{10... | collective-permute-start | bytes 307208 | tf_op jit(solution)/shard_map/ppermute | solution.py:423
  47.8 2.2 %collective-permute-start.7 = (bf16[9,16,128]{2,1,0:T(8,128)(2,1)S(1)}, bf16[9,16,128]{2,1,0:T(8,128)(2,1)S(1)}, u32[]{:S(2)}, u32[]{:S(2)}) collective-permute-start(bf16[9,16,128]{2,1,0:T(8,128)(2,1)S(1)} %add_convert_fusion.half), channel_id=1, source_target_pairs={{0,1},{1,0},{2,3},{3,2},{4,5},{5,4},{6,7},{7,6},{8,9},{9,8},{10,11... | collective-permute-start | bytes 110600 | tf_op jit(solution)/shard_map/ppermute | solution.py:423
where the time goes:
time: 50.9 us; the launch traced here: 50.6 us
  Pallas kernels  29.6 us (58%)
  starting transfers between devices  14.7 us (29%)
  waiting for transfers between devices  5.16 us (10%)
  between operations  0.89 us (2%)
    ppermute x5, starting transfers between devices, shifted(): lax.ppermute(value, axis, [(source, source + steps) for source in range(f...  10.1 us
    pallas_call x1, Pallas kernels, per_device(): call(sums_kernel, 'sums', [twice(wide)] * 7 + [twice(chunk), twice(chunk)...  8.48 us
    ppermute x3, starting transfers between devices, swapped(): lax.ppermute(value, axis, [(source, source ^ bit) for source in range(cou...  4.61 us
    ppermute x5, waiting for transfers between devices, shifted(): lax.ppermute(value, axis, [(source, source + steps) for source in range(f...  3.97 us
    pallas_call x1, Pallas kernels, per_device(): call(product_kernel, 'product', [wide, wide, table, wide, wide], [wide, w...  3.67 us
    pallas_call x1, Pallas kernels, per_device(): call(forward_kernel, 'forward', [wide, wide, table, wide, wide, wide], [w...  3.38 us
    pallas_call x1, Pallas kernels, per_device(): call(functools.partial(within_kernel, bits), 'within', [wide, table, chun...  3.11 us
    pallas_call x1, Pallas kernels, per_device(): call(local_kernel, 'local', [wide, wide, table], [wide], [wide_full])  2.26 us
  transfers between devices with their start and end apart: 8, of which 3 were waited for; matrix products, arithmetic and copies ran while one was open for 0% of the time, Pallas kernels for 51%

commit v1 on v0

--- a/solution.py
+++ b/solution.py
@@ -123,10 +123,8 @@
     sums = jnp.where(lanes + rows < CHUNK, wide[:, TILE:], wide[:, :TILE])
     parts = []
     for start in (0, CHUNK):
-        total = sums[start : start + 8]
-        for turn in (8, 16, 24):
-            total = total + pltpu.roll(sums[start + turn : start + turn + 8], turn, 1)
-        parts.append(pltpu.roll(total, 0, 1, stride=1, stride_axis=0))
+        part = pltpu.roll(sums[start : start + CHUNK], 0, 1, stride=1, stride_axis=0)
+        parts.append(part[:8] + part[8:16] + part[16:24] + part[24:])
     return above(*parts).astype(BF16)
 
 
@@ -264,11 +262,34 @@
         dz1[span, :] = (dy1 * value[span, :].astype(F32)).astype(BF16)
 
 
-def forward_kernel(before, now, filters, value, li_key, to_end, z1, u2, state):
+def forward_kernel(
+    before, now, filters, value, li_key, to_end, dz1, grad, li_value, power, after_shard, rate,
+    z1, u2, packed, filter_sums, within_sums, across_sums,
+):
     rows, cols = iotas()
     mask = rows // LANES == cols // LANES
     upper = ones_where(cols >= rows)
     upper_half = beside(upper, upper)
+    turn = ones_where(cols == rows - rows % CHUNK + (CHUNK - 1 - rows % CHUNK))
+    lanes = lax.broadcasted_iota(jnp.int32, (CHUNK, TILE), 1)
+    own_rows = [ones_where((lanes // LANES) % 2 == i) for i in range(2)]
+    eights = ones_where(
+        lax.broadcasted_iota(jnp.int32, (2 * PACK, TILE), 1) // 8
+        == lax.broadcasted_iota(jnp.int32, (2 * PACK, TILE), 0)
+    )
+    at = pl.program_id(0)
+    blocks = now.shape[0] // TILE
+
+    @pl.when(at == 0)
+    def _():
+        within_sums[...] = jnp.zeros_like(within_sums)
+        across_sums[...] = jnp.zeros_like(across_sums)
+
+    turned = []
+    for span in spans(now):
+        dz2 = grad[span, :] * li_value[span, :]
+        turned.append(nt(turn, above(dz1[span, :], dz2)).astype(BF16))
+    chunks = [(pair_chunks(each[:, :TILE]), pair_chunks(each[:, TILE:])) for each in turned]
     results = [
         now_and_before(
             now[span, :], before[span, :], group_rows(filters, block).astype(F32), upper_half
@@ -277,58 +298,33 @@
     ]
     halves = []
     for span, result in zip(spans(now), results):
+        z1[span, :] = result
         y1 = (value[span, :].astype(F32) * result).astype(BF16).astype(F32)
         halves.append((y1 * li_key[span, :].astype(F32)).astype(BF16))
+        u2[span, :] = halves[-1]
     ends = [nt(to_end[span, :], half) for span, half in zip(spans(now), halves)]
-    for block, span in enumerate(spans(now)):
-        z1[span, :] = results[block]
-        u2[span, :] = halves[block]
-        state[block] = squeeze_groups(ends[block], mask).astype(BF16)
-
-
-def sums_kernel(
-    before, now, u2, dz1, grad, li_value, power, state, after_shard, rate,
-    packed, filter_sums, within_sums, across_sums,
-):
-    rows, cols = iotas()
-    turn = ones_where(cols == rows - rows % CHUNK + (CHUNK - 1 - rows % CHUNK))
-    lanes = lax.broadcasted_iota(jnp.int32, (CHUNK, TILE), 1)
-    own_rows = [ones_where((lanes // LANES) % 2 == i) for i in range(2)]
-    at = pl.program_id(0)
-    blocks = now.shape[0] // TILE
-
-    @pl.when(at == 0)
-    def _():
-        within_sums[...] = jnp.zeros_like(within_sums)
-        across_sums[...] = jnp.zeros_like(across_sums)
-
-    eights = ones_where(
-        lax.broadcasted_iota(jnp.int32, (2 * PACK, TILE), 1) // 8
-        == lax.broadcasted_iota(jnp.int32, (2 * PACK, TILE), 0)
-    )
-    turned = []
-    for span in spans(now):
-        dz2 = grad[span, :] * li_value[span, :]
-        turned.append(nt(turn, above(dz1[span, :], dz2)).astype(BF16))
-    chunks = [(pair_chunks(each[:, :TILE]), pair_chunks(each[:, TILE:])) for each in turned]
-    lags, energies = [], []
+
+    lags = []
     for block in range(blocks):
         lag, energy = [], []
         for p in range(TILE // CHUNK):
             pair = pl.ds(block * TILE + p * CHUNK, CHUNK)
             older, newer = before[pair, :], now[pair, :]
+            later = halves[block][p * CHUNK : (p + 1) * CHUNK]
             lag.append(lag_rows(chunks[block][0][p], windows(older, newer), own_rows))
-            energy.append(lag_rows(chunks[block][1][p], windows(None, u2[pair, :]), own_rows))
-        both = nn(eights, above(*lag, *energy))
-        lags.append(both[:PACK])
-        energies.append(above(*[both[PACK:].astype(BF16)] * LANES))
+            energy.append(lag_rows(chunks[block][1][p], windows(None, later), own_rows))
+        lags.append(above(*lag, *energy))
+    lags = [nn(eights, each) for each in lags]
     within, across = jnp.zeros((LANES, TILE), F32), jnp.zeros((LANES, TILE), F32)
     for block, span in enumerate(spans(now)):
         own = block_groups(at, blocks, block)
-        within = within + squeeze_groups(nt(power[span, :], energies[block]), own)
-        crossing = state[block].astype(F32) * after_shard[block]
+        energies = above(*[lags[block][PACK:].astype(BF16)] * LANES)
+        within = within + squeeze_groups(nt(power[span, :], energies), own)
+        state = squeeze_groups(ends[block], mask).astype(BF16)
+        crossing = state.astype(F32) * after_shard[block]
         across = across + nn(crossing.astype(BF16), ones_where(own))
-        packed[at * blocks + block] = state[block]
+        packed[at * blocks + block] = state
+    lags = [each[:PACK] for each in lags]
     few = blocks * PACK
     filter_sums[pl.ds(pl.multiple_of(at * few, few), few), :] = above(*lags)
     within_sums[...] += within
@@ -403,13 +399,27 @@
         grad_key[span, :] = (du1 * query[span, :].astype(F32)).astype(BF16)
 
 
-def value_kernel(states, after, z2, grad, grad_value):
+def value_kernel(states, after, z2, grad, grad_value, made, left):
     rows, cols = iotas()
     mask = rows // LANES == cols // LANES
+    at = pl.program_id(0)
+    size = z2.shape[0]
+
+    def store(step):
+        span = pl.ds(pl.multiple_of(step * size, size), size)
+        return pltpu.make_async_copy(made.at[span, :], grad_value.at[span, :], left.at[step])
+
     wides = [spread_groups(states[block], mask).T.astype(BF16) for block in range(states.shape[0])]
     totals = [z2[span, :] + nn(wide, after[span, :]) for span, wide in zip(spans(z2), wides)]
-    for span, total in zip(spans(z2), totals):
-        grad_value[span, :] = (grad[span, :].astype(F32) * total).astype(BF16)
+    for block, (span, total) in enumerate(zip(spans(z2), totals)):
+        here = pl.ds(pl.multiple_of(at * size + block * TILE, TILE), TILE)
+        made[here, :] = (grad[span, :].astype(F32) * total).astype(BF16)
+    store(at).start()
+
+    @pl.when(at == STEPS - 1)
+    def _():
+        for step in range(STEPS):
+            store(step).wait()
 
 
 def shifted(value, axis, steps):
@@ -520,21 +530,18 @@
     )(after_shard, du2_local, to_next, key_two, value, product_before)
     dz1_later = shifted(dz1, "seq", -1)
 
-    z1, u2, state = call(
-        forward_kernel, "forward",
-        [wide, wide, table, wide, wide, wide],
-        [wide, wide, chunk], [wide_full, wide_half, chunk_half],
-    )(product_before, product, mr_filter, value, key_two, to_end)
-
     filter_chunks = groups // LANES
     packed_shape = jax.ShapeDtypeStruct((blocks + filter_chunks + 1, LANES, TILE), BF16)
-    (packed,) = call(
-        sums_kernel, "sums",
-        [twice(wide)] * 7 + [twice(chunk), twice(chunk), modes],
-        [whole(packed_shape)], [packed_shape],
+    z1, u2, packed = call(
+        forward_kernel, "forward",
+        [twice(spec) for spec in [wide, wide, table] + [wide] * 7 + [chunk]] + [modes],
+        [twice(wide), twice(wide), whole(packed_shape)], [wide_full, wide_half, packed_shape],
         [pltpu.VMEM((groups, TILE), F32)] + [pltpu.VMEM((LANES, TILE), F32)] * 2,
         grid=STEPS // 2,
-    )(product_before, product, u2, dz1, grad, value_two, power, state, after_shard, rate)
+    )(
+        product_before, product, mr_filter, value, key_two, to_end, dz1, grad, value_two, power,
+        after_shard, rate,
+    )
 
     bits = scan_bits()
     few_full = jax.ShapeDtypeStruct((filter_chunks + 1, LANES, TILE), F32)
@@ -569,7 +576,8 @@
     assert lax.axis_size("dp") == 2
     partner = swapped(sums, "dp", 1)
     (grad_li_value,) = call(
-        value_kernel, "value", [chunk, wide, wide, wide], [wide], [wide_half]
+        value_kernel, "value", [chunk, wide, wide, wide], [distant], [wide_half],
+        [pltpu.VMEM((channels, TILE), BF16), pltpu.SemaphoreType.DMA((STEPS,))],
     )(before_shard, after, z2, grad)
 
     residue_full = jax.ShapeDtypeStruct((LANES, TILE), F32)

time: 50.9 us -> 49.6 us (0.974)
  Pallas kernels: 29.6 us -> 23.7 us
  waiting for transfers between devices: 5.16 us -> 9.29 us
    pallas_call x3 -> x2, Pallas kernels: 14 us -> 8.1 us  [the longest x1 6.34 us: per_device(): call(forward_kernel, 'forward', [twice(spec) for spec in [wide, wide, tab...]
    ppermute x5, waiting for transfers between devices: 3.97 us -> 8.99 us  [shifted(): lax.ppermute(value, axis, [(source, source + steps) for source in range(f...]
    ppermute x3, waiting for transfers between devices: 1.19 us -> 0.3 us  [swapped(): lax.ppermute(value, axis, [(source, source ^ bit) for source in range(cou...]
  transfers between devices with their start and end apart: 8 -> 8, of which waited for: 3 -> 4; matrix products, arithmetic and copies ran while one was open for 0% -> 0% of each run, Pallas kernels for 51% -> 40%
where the time goes in v1:
time: 49.6 us; the launch traced here: 49.3 us
  Pallas kernels  23.7 us (48%)
  starting transfers between devices  15.2 us (31%)
  waiting for transfers between devices  9.29 us (19%)
  between operations  0.9 us (2%)
    ppermute x5, starting transfers between devices, shifted(): lax.ppermute(value, axis, [(source, source + steps) for source in range(f...  10.1 us
    ppermute x5, waiting for transfers between devices, shifted(): lax.ppermute(value, axis, [(source, source + steps) for source in range(f...  8.99 us
    pallas_call x1, Pallas kernels, per_device(): call(forward_kernel, 'forward', [twice(spec) for spec in [wide, wide, tab...  6.34 us
    ppermute x3, starting transfers between devices, swapped(): lax.ppermute(value, axis, [(source, source ^ bit) for source in range(cou...  5.03 us
    pallas_call x1, Pallas kernels, per_device(): call(product_kernel, 'product', [wide, wide, table, wide, wide], [wide, w...  3.68 us
    pallas_call x1, Pallas kernels, per_device(): call(functools.partial(within_kernel, bits), 'within', [wide, table, chun...  3.09 us
    pallas_call x1, Pallas kernels, per_device(): call(local_kernel, 'local', [wide, wide, table], [wide], [wide_full])  2.26 us
    pallas_call x1, Pallas kernels, per_device(): call(gate_kernel, 'gate', [distant] * 2, [distant], [wide_half], [pltpu.V...  2.15 us
  transfers between devices with their start and end apart: 8, of which 4 were waited for; matrix products, arithmetic and copies ran while one was open for 0% of the time, Pallas kernels for 40%

profile of v1, /device:TPU:0, one launch (start us, length us, event | category | flops | bytes accessed | tf_op | source)
XLA Modules:
  0.0 49.3 jit_solution(17546600601329110403)
XLA Ops:
  0.6 0.0 copy-start
  0.6 0.0 copy-start.3
  0.7 0.0 copy-start.8
  0.7 2.1 %gate.1.now = bf16[2048,128]{1,0:T(8,128)(2,1)} custom-call(bf16[2048,128]{1,0:T(8,128)(2,1)} %bitcast.27, bf16[2048,128]{1,0:T(8,128)(2,1)} %bitcast.29), custom_call_target="tpu_custom_call" | custom-call | bytes 1 | tf_op jit(solution)/shard_map/gate/pallas_call | solution.py:496
  2.8 5.0 %collective-permute-start.3 = (bf16[2048,128]{1,0:T(8,128)(2,1)}, bf16[2048,128]{1,0:T(8,128)(2,1)S(1)}, u32[]{:S(2)}, u32[]{:S(2)}) collective-permute-start(bf16[2048,128]{1,0:T(8,128)(2,1)} %gate.1.now), channel_id=1, source_target_pairs={{0,8},{8,16},{16,24},{1,9},{9,17},{17,25},{2,10},{10,18},{18,26},{... | collective-permute-start | bytes 1572872 | tf_op jit(solution)/shard_map/ppermute | solution.py:428
  7.8 0.0 copy-done
  7.8 0.0 copy-done.3
  7.8 0.0 copy-done.8
  7.8 0.0 copy-start.7
  7.8 0.0 copy-start.9
  7.8 1.2 %state.1 = bf16[16,16,128]{2,1,0:T(8,128)(2,1)S(1)} custom-call(bf16[2048,128]{1,0:T(8,128)(2,1)S(1)} %bitcast.14, bf16[2048,128]{1,0:T(8,128)(2,1)S(1)} %bitcast.24, f32[16,128]{1,0:T(8,128)S(1)} %bitcast.31), custom_call_target="tpu_custom_call" | custom-call | bytes 1 | tf_op jit(solution)/shard_map/state/pallas_call | solution.py:506
  9.0 1.3 %collective-permute-start = (bf16[16,16,128]{2,1,0:T(8,128)(2,1)S(1)}, bf16[16,16,128]{2,1,0:T(8,128)(2,1)S(1)}, u32[]{:S(2)}, u32[]{:S(2)}) collective-permute-start(bf16[16,16,128]{2,1,0:T(8,128)(2,1)S(1)} %state.1), channel_id=1, source_target_pairs={{8,0},{16,8},{24,16},{9,1},{17,9},{25,17},{10,2},{18,10},{26,18},{... | collective-permute-start | bytes 196616 | tf_op jit(solution)/shard_map/ppermute | solution.py:428
  10.3 1.3 %collective-permute-start.1 = (bf16[16,16,128]{2,1,0:T(8,128)(2,1)S(1)}, bf16[16,16,128]{2,1,0:T(8,128)(2,1)S(1)}, u32[]{:S(2)}, u32[]{:S(2)}) collective-permute-start(bf16[16,16,128]{2,1,0:T(8,128)(2,1)S(1)} %state.1), channel_id=1, source_target_pairs={{16,0},{24,8},{17,1},{25,9},{18,2},{26,10},{19,3},{27,11},{20,4},{... | collective-permute-start | bytes 196616 | tf_op jit(solution)/shard_map/ppermute | solution.py:428
  11.6 1.3 %collective-permute-start.2 = (bf16[16,16,128]{2,1,0:T(8,128)(2,1)S(1)}, bf16[16,16,128]{2,1,0:T(8,128)(2,1)S(1)}, u32[]{:S(2)}, u32[]{:S(2)}) collective-permute-start(bf16[16,16,128]{2,1,0:T(8,128)(2,1)S(1)} %state.1), channel_id=1, source_target_pairs={{24,0},{25,1},{26,2},{27,3},{28,4},{29,5},{30,6},{31,7}} | collective-permute-start | bytes 196616 | tf_op jit(solution)/shard_map/ppermute | solution.py:428
  12.9 0.0 copy-done.7
  12.9 0.0 copy-done.9
  12.9 1.6 %table.1 = (bf16[2048,128]{1,0:T(8,128)(2,1)S(1)}, bf16[2048,128]{1,0:T(8,128)(2,1)S(1)}, bf16[2048,128]{1,0:T(8,128)(2,1)S(1)}, bf16[2048,128]{1,0:T(8,128)(2,1...) custom-call(f32[16,128]{1,0:T(8,128)S(1)} %bitcast.32, ...), custom_call_target="tpu_custom_call" | custom-call | bytes 1 | tf_op jit(solution)/shard_map/table/pallas_call | solution.py:511
  14.5 0.0 copy-start.1
  14.5 0.0 copy-start.2
  14.5 2.3 %local.1 = f32[2048,128]{1,0:T(8,128)S(1)} custom-call(bf16[2048,128]{1,0:T(8,128)(2,1)S(1)} %bitcast.15, bf16[2048,128]{1,0:T(8,128)(2,1)S(1)} %bitcast.25, f32[128,128]{1,0:T(8,128)S(1)} %get-tuple-element.34.turned), custom_call_target="tpu_custom_call" | custom-call | bytes 1 | tf_op jit(solution)/shard_map/local/pallas_call | solution.py:521
  16.8 0.0 collective-permute-done
  16.8 1.4 %collective-permute-done.1 = bf16[16,16,128]{2,1,0:T(8,128)(2,1)S(1)} collective-permute-done((bf16[16,16,128]{2,1,0:T(8,128)(2,1)S(1)}, bf16[16,16,128]{2,1,0:T(8,128)(2,1)S(1)}, u32[]{:S(2)}, u32[]{:S(2)}) %collective-permute-start.1) | collective-permute-done | bytes 65568 | tf_op jit(solution)/shard_map/ppermute | solution.py:428
  18.2 2.6 %collective-permute-done.2 = bf16[16,16,128]{2,1,0:T(8,128)(2,1)S(1)} collective-permute-done((bf16[16,16,128]{2,1,0:T(8,128)(2,1)S(1)}, bf16[16,16,128]{2,1,0:T(8,128)(2,1)S(1)}, u32[]{:S(2)}, u32[]{:S(2)}) %collective-permute-start.2) | collective-permute-done | bytes 65568 | tf_op jit(solution)/shard_map/ppermute | solution.py:428
  20.7 0.1 exponential_multiply_fusion.states.after_shard
  20.8 0.0 collective-permute-done.3.before
  20.8 0.0 copy-done.1
  20.8 0.0 copy-done.2
  20.8 0.0 copy-start.4
  20.9 1.1 %middle.1 = (bf16[2048,128]{1,0:T(8,128)(2,1)S(1)}, f32[2048,128]{1,0:T(8,128)S(1)}) custom-call(f32[16,16,128]{2,1,0:T(8,128)S(1)} %exponential_multiply_fusion.states.after_shard, f32[2048,128]{1,0:T(8,128)S(1)} %local.1, bf16[2048,128]{1,0:T(8,128)(2,1)S(1)} %get-tuple-element.35.to_next, bf16[2048,128]{1,0:T(8,128)(2,1)S(1)} %bitcast.18, ...), custom_call_target="tpu_custom_call" | custom-call | bytes 1 | tf_op jit(solution)/shard_map/middle/pallas_call | solution.py:527
  22.0 1.3 %collective-permute-start.4 = (bf16[2048,128]{1,0:T(8,128)(2,1)S(1)}, bf16[2048,128]{1,0:T(8,128)(2,1)S(1)}, u32[]{:S(2)}, u32[]{:S(2)}) collective-permute-start(bf16[2048,128]{1,0:T(8,128)(2,1)S(1)} %get-tuple-element.36.dz1), channel_id=1, source_target_pairs={{8,0},{16,8},{24,16},{9,1},{17,9},{25,17},{10,2},{18,10},{26,18},{... | collective-permute-start | bytes 1572872 | tf_op jit(solution)/shard_map/ppermute | solution.py:428
  23.3 0.0 copy-done.4
  23.3 6.3 %forward.1 = (f32[2048,128]{1,0:T(8,128)S(1)}, bf16[2048,128]{1,0:T(8,128)(2,1)S(1)}, bf16[25,16,128]{2,1,0:T(8,128)(2,1)S(1)}) custom-call(bf16[2048,128]{1,0:T(8,128)(2,1)S(1)} %collective-permute-done.3.before, bf16[2048,128]{1,0:T(8,128)(2,1)S(1)} %copy-done.4, bf16[128,128]{1,0:T(8,128)(2,1)S(1)} %copy-done.7, bf16[2048,128]{1,0:T(8,128)(2,1)S(1)} %bitcast.22, ...), custom_call_target="tpu_custom_call" | custom-call | bytes 1 | tf_op jit(solution)/shard_map/forward/pallas_call | solution.py:535
  29.6 2.7 %collective-permute-start.5 = (bf16[25,16,128]{2,1,0:T(8,128)(2,1)S(1)}, bf16[25,16,128]{2,1,0:T(8,128)(2,1)S(1)}, u32[]{:S(2)}, u32[]{:S(2)}) collective-permute-start(bf16[25,16,128]{2,1,0:T(8,128)(2,1)S(1)} %get-tuple-element.49), channel_id=1, source_target_pairs={{0,8},{8,0},{16,24},{24,16},{1,9},{9,1},{17,25},{25,17},{2,10},{10... | collective-permute-start | bytes 307208 | tf_op jit(solution)/shard_map/ppermute | solution.py:433
  32.3 5.0 %collective-permute-done.4.later = bf16[2048,128]{1,0:T(8,128)(2,1)S(1)} collective-permute-done((bf16[2048,128]{1,0:T(8,128)(2,1)S(1)}, bf16[2048,128]{1,0:T(8,128)(2,1)S(1)}, u32[]{:S(2)}, u32[]{:S(2)}) %collective-permute-start.4) | collective-permute-done | bytes 524320 | tf_op jit(solution)/shard_map/ppermute | solution.py:428
  37.3 0.0 copy-start.6
  37.3 3.1 %within.1 = (f32[2048,128]{1,0:T(8,128)S(1)}, bf16[2048,128]{1,0:T(8,128)(2,1)}, bf16[2048,128]{1,0:T(8,128)(2,1)}, f32[9,16,128]{2,1,0:T(8,128)S(1)}, f32[16,16...) custom-call(bf16[2048,128]{1,0:T(8,128)(2,1)S(1)} %get-tuple-element.42, ...), custom_call_target="tpu_custom_call" | custom-call | bytes 1 | tf_op jit(solution)/shard_map/within/pallas_call | solution.py:549
  40.4 0.0 copy-start.5
  40.4 0.0 collective-permute-done.5
  40.5 2.3 %collective-permute-start.6 = (bf16[25,16,128]{2,1,0:T(8,128)(2,1)S(1)}, bf16[25,16,128]{2,1,0:T(8,128)(2,1)S(1)}, u32[]{:S(2)}, u32[]{:S(2)}) collective-permute-start(bf16[25,16,128]{2,1,0:T(8,128)(2,1)S(1)} %pad_maximum_fusion), channel_id=1, source_target_pairs={{0,16},{8,24},{16,0},{24,8},{1,17},{9,25},{17,1},{25,9},{2,18},{10... | collective-permute-start | bytes 307208 | tf_op jit(solution)/shard_map/ppermute | solution.py:433
  42.8 0.0 copy-done.6
  42.8 0.0 copy-done.5
  42.8 3.7 %product.1 = (bf16[2048,128]{1,0:T(8,128)(2,1)}, bf16[2048,128]{1,0:T(8,128)(2,1)}, f32[9,16,128]{2,1,0:T(8,128)S(1)}) custom-call(bf16[2048,128]{1,0:T(8,128)(2,1)S(1)} %get-tuple-element.36.dz1, bf16[2048,128]{1,0:T(8,128)(2,1)S(1)} %collective-permute-done.4.later, f32[128,128]{1,0:T(8,128)S(1)} %get-tuple-element.37.turned, ...), custom_call_target="tpu_custom_call" | custom-call | bytes 1 | tf_op jit(solution)/shard_map/product/pallas_call | solution.py:556
  46.4 0.3 collective-permute-done.6
  46.8 0.1 collective-permute-start.7
  46.9 1.8 %value.1 = bf16[2048,128]{1,0:T(8,128)(2,1)} custom-call(f32[16,16,128]{2,1,0:T(8,128)S(1)} %fusion.states, bf16[2048,128]{1,0:T(8,128)(2,1)S(1)} %get-tuple-element.54.after, f32[2048,128]{1,0:T(8,128)S(1)} %get-tuple-element.55.z2, bf16[2048,128]{1,0:T(8,128)(2,1)S(1)} %bitcast.17), custom_call_target="tpu_custom_call" | custom-call | bytes 1 | tf_op jit(solution)/shard_map/value/pallas_call | solution.py:578
  48.7 0.0 collective-permute-done.7.other
  48.7 0.6 %last.1 = (f32[128,128]{1,0:T(8,128)}, f32[16,128]{1,0:T(8,128)}) custom-call(bf16[9,16,128]{2,1,0:T(8,128)(2,1)S(1)} %add_convert_fusion.half, bf16[9,16,128]{2,1,0:T(8,128)(2,1)S(1)} %collective-permute-done.7.other), custom_call_target="tpu_custom_call" | custom-call | bytes 1 | tf_op jit(solution)/shard_map/last/pallas_call | solution.py:584
  (5 shorter events, 0.1 us)
Async XLA Ops:
  0.6 7.2 %copy-start = (bf16[1,2048,128]{2,1,0:T(8,128)(2,1)S(1)}, bf16[1,2048,128]{2,1,0:T(8,128)(2,1)}, u32[]{:S(2)}) copy-start(bf16[1,2048,128]{2,1,0:T(8,128)(2,1)} %param.14) | copy-start | bytes 1572868
  0.6 7.2 %copy-start.3 = (bf16[1,2048,128]{2,1,0:T(8,128)(2,1)S(1)}, bf16[1,2048,128]{2,1,0:T(8,128)(2,1)}, u32[]{:S(2)}) copy-start(bf16[1,2048,128]{2,1,0:T(8,128)(2,1)} %param.13) | copy-start | bytes 1572868
  0.7 7.2 %copy-start.8 = (f32[128,16]{0,1:T(8,128)S(1)}, f32[128,16]{0,1:T(8,128)}, u32[]{:S(2)}) copy-start(f32[128,16]{0,1:T(8,128)} %param.17) | copy-start | bytes 24580
  2.8 18.0 %collective-permute-start.3 = (bf16[2048,128]{1,0:T(8,128)(2,1)}, bf16[2048,128]{1,0:T(8,128)(2,1)S(1)}, u32[]{:S(2)}, u32[]{:S(2)}) collective-permute-start(bf16[2048,128]{1,0:T(8,128)(2,1)} %gate.1.now), channel_id=1, source_target_pairs={{0,8},{8,16},{16,24},{1,9},{9,17},{17,25},{2,10},{10,18},{18,26},{... | collective-permute-start | bytes 1572872 | tf_op jit(solution)/shard_map/ppermute | solution.py:428
  7.8 5.1 %copy-start.7 = (bf16[128,128]{1,0:T(8,128)(2,1)S(1)}, bf16[128,128]{1,0:T(8,128)(2,1)}, u32[]{:S(2)}) copy-start(bf16[128,128]{1,0:T(8,128)(2,1)} %filters.3) | copy-start | bytes 98308
  7.8 5.1 %copy-start.9 = (f32[128,16]{0,1:T(8,128)S(1)}, f32[128,16]{0,1:T(8,128)}, u32[]{:S(2)}) copy-start(f32[128,16]{0,1:T(8,128)} %param.16) | copy-start | bytes 24580
  9.0 7.8 %collective-permute-start = (bf16[16,16,128]{2,1,0:T(8,128)(2,1)S(1)}, bf16[16,16,128]{2,1,0:T(8,128)(2,1)S(1)}, u32[]{:S(2)}, u32[]{:S(2)}) collective-permute-start(bf16[16,16,128]{2,1,0:T(8,128)(2,1)S(1)} %state.1), channel_id=1, source_target_pairs={{8,0},{16,8},{24,16},{9,1},{17,9},{25,17},{10,2},{18,10},{26,18},{... | collective-permute-start | bytes 196616 | tf_op jit(solution)/shard_map/ppermute | solution.py:428
  10.3 7.8 %collective-permute-start.1 = (bf16[16,16,128]{2,1,0:T(8,128)(2,1)S(1)}, bf16[16,16,128]{2,1,0:T(8,128)(2,1)S(1)}, u32[]{:S(2)}, u32[]{:S(2)}) collective-permute-start(bf16[16,16,128]{2,1,0:T(8,128)(2,1)S(1)} %state.1), channel_id=1, source_target_pairs={{16,0},{24,8},{17,1},{25,9},{18,2},{26,10},{19,3},{27,11},{20,4},{... | collective-permute-start | bytes 196616 | tf_op jit(solution)/shard_map/ppermute | solution.py:428
  11.6 9.1 %collective-permute-start.2 = (bf16[16,16,128]{2,1,0:T(8,128)(2,1)S(1)}, bf16[16,16,128]{2,1,0:T(8,128)(2,1)S(1)}, u32[]{:S(2)}, u32[]{:S(2)}) collective-permute-start(bf16[16,16,128]{2,1,0:T(8,128)(2,1)S(1)} %state.1), channel_id=1, source_target_pairs={{24,0},{25,1},{26,2},{27,3},{28,4},{29,5},{30,6},{31,7}} | collective-permute-start | bytes 196616 | tf_op jit(solution)/shard_map/ppermute | solution.py:428
  14.5 6.3 %copy-start.1 = (bf16[1,2048,128]{2,1,0:T(8,128)(2,1)S(1)}, bf16[1,2048,128]{2,1,0:T(8,128)(2,1)}, u32[]{:S(2)}) copy-start(bf16[1,2048,128]{2,1,0:T(8,128)(2,1)} %param.12) | copy-start | bytes 1572868
  14.5 6.3 %copy-start.2 = (bf16[1,2048,128]{2,1,0:T(8,128)(2,1)S(1)}, bf16[1,2048,128]{2,1,0:T(8,128)(2,1)}, u32[]{:S(2)}) copy-start(bf16[1,2048,128]{2,1,0:T(8,128)(2,1)} %param.11) | copy-start | bytes 1572868
  20.8 2.4 %copy-start.4 = (bf16[2048,128]{1,0:T(8,128)(2,1)S(1)}, bf16[2048,128]{1,0:T(8,128)(2,1)}, u32[]{:S(2)}) copy-start(bf16[2048,128]{1,0:T(8,128)(2,1)} %gate.1.now) | copy-start | bytes 1572868
  22.0 15.3 %collective-permute-start.4 = (bf16[2048,128]{1,0:T(8,128)(2,1)S(1)}, bf16[2048,128]{1,0:T(8,128)(2,1)S(1)}, u32[]{:S(2)}, u32[]{:S(2)}) collective-permute-start(bf16[2048,128]{1,0:T(8,128)(2,1)S(1)} %get-tuple-element.36.dz1), channel_id=1, source_target_pairs={{8,0},{16,8},{24,16},{9,1},{17,9},{25,17},{10,2},{18,10},{26,18},{... | collective-permute-start | bytes 1572872 | tf_op jit(solution)/shard_map/ppermute | solution.py:428
  29.6 10.8 %collective-permute-start.5 = (bf16[25,16,128]{2,1,0:T(8,128)(2,1)S(1)}, bf16[25,16,128]{2,1,0:T(8,128)(2,1)S(1)}, u32[]{:S(2)}, u32[]{:S(2)}) collective-permute-start(bf16[25,16,128]{2,1,0:T(8,128)(2,1)S(1)} %get-tuple-element.49), channel_id=1, source_target_pairs={{0,8},{8,0},{16,24},{24,16},{1,9},{9,1},{17,25},{25,17},{2,10},{10... | collective-permute-start | bytes 307208 | tf_op jit(solution)/shard_map/ppermute | solution.py:433
  37.3 5.5 %copy-start.6 = (bf16[1,2048,128]{2,1,0:T(8,128)(2,1)S(1)}, bf16[1,2048,128]{2,1,0:T(8,128)(2,1)}, u32[]{:S(2)}) copy-start(bf16[1,2048,128]{2,1,0:T(8,128)(2,1)} %param.10) | copy-start | bytes 1572868
  40.4 2.4 %copy-start.5 = (bf16[1,2048,128]{2,1,0:T(8,128)(2,1)S(1)}, bf16[1,2048,128]{2,1,0:T(8,128)(2,1)}, u32[]{:S(2)}) copy-start(bf16[1,2048,128]{2,1,0:T(8,128)(2,1)} %param.9) | copy-start | bytes 1572868
  40.5 6.3 %collective-permute-start.6 = (bf16[25,16,128]{2,1,0:T(8,128)(2,1)S(1)}, bf16[25,16,128]{2,1,0:T(8,128)(2,1)S(1)}, u32[]{:S(2)}, u32[]{:S(2)}) collective-permute-start(bf16[25,16,128]{2,1,0:T(8,128)(2,1)S(1)} %pad_maximum_fusion), channel_id=1, source_target_pairs={{0,16},{8,24},{16,0},{24,8},{1,17},{9,25},{17,1},{25,9},{2,18},{10... | collective-permute-start | bytes 307208 | tf_op jit(solution)/shard_map/ppermute | solution.py:433
  46.8 1.9 %collective-permute-start.7 = (bf16[9,16,128]{2,1,0:T(8,128)(2,1)S(1)}, bf16[9,16,128]{2,1,0:T(8,128)(2,1)S(1)}, u32[]{:S(2)}, u32[]{:S(2)}) collective-permute-start(bf16[9,16,128]{2,1,0:T(8,128)(2,1)S(1)} %add_convert_fusion.half), channel_id=1, source_target_pairs={{0,1},{1,0},{2,3},{3,2},{4,5},{5,4},{6,7},{7,6},{8,9},{9,8},{10,11... | collective-permute-start | bytes 110600 | tf_op jit(solution)/shard_map/ppermute | solution.py:433

commit v2 on v1

--- a/solution.py
+++ b/solution.py
@@ -343,10 +343,7 @@
         packed[steps * blocks + filter_sums.shape[0] // LANES] = total.astype(BF16)
 
 
-def within_kernel(
-    bits, u2, taps, wide_rate, z1, du2, value, li_key, later,
-    z2, grad_value, grad_key, zeros, *weights,
-):
+def factor_kernel(bits, wide_rate, later, zeros, *weights):
     zeros[...] = jnp.zeros_like(zeros)
     place = lax.axis_index("seq")
     rates = wide_rate[...]
@@ -361,6 +358,10 @@
             one = jnp.ones_like(run)
             weights.pop(0)[...] = jnp.where(high, run, one)
             weights.pop(0)[...] = jnp.where(high, one, run)
+
+
+def within_kernel(u2, taps, z1, du2, value, li_key, z2, grad_value, grad_key, zeros):
+    zeros[...] = jnp.zeros_like(zeros)
     rows, cols = iotas()
     upper = ones_where(cols >= rows)
     upper_half = beside(upper, upper)
@@ -546,20 +547,26 @@
     bits = scan_bits()
     few_full = jax.ShapeDtypeStruct((filter_chunks + 1, LANES, TILE), F32)
     factors = 3 * len(bits) - 2
-    z2, grad_mr_value, grad_li_key, within_zeros, *weights = call(
-        functools.partial(within_kernel, bits), "within",
-        [wide, table, chunk, wide, wide, wide, wide, anywhere],
-        [wide, wide, wide, whole(few_full)] + [chunk] * factors,
-        [wide_full, wide_half, wide_half, few_full] + [chunk_full] * factors,
-    )(u2, taps, wide_rate, z1, du2, value, key_two, dz1_later)
+    z2, grad_mr_value, grad_li_key, within_zeros = call(
+        within_kernel, "within",
+        [wide, table, wide, wide, wide, wide], [wide] * 3 + [whole(few_full)],
+        [wide_full, wide_half, wide_half, few_full],
+    )(u2, taps, z1, du2, value, key_two)
+
+    factor_zeros, *weights = call(
+        functools.partial(factor_kernel, bits), "factor", [whole(chunk_full), anywhere],
+        [whole(few_full)] + [whole(chunk_full)] * factors, [few_full] + [chunk_full] * factors,
+        grid=1,
+    )(wide_rate, dz1_later)
 
     grad_query, grad_key, product_zeros = call(
         product_kernel, "product",
-        [wide, wide, table, wide, wide], [wide, wide, whole(few_full)],
-        [wide_half, wide_half, few_full],
+        [twice(spec) for spec in (wide, wide, table, wide, wide)],
+        [twice(wide), twice(wide), whole(few_full)], [wide_half, wide_half, few_full],
+        grid=STEPS // 2,
     )(dz1, dz1_later, mr_turned, query, key)
 
-    zeros = [within_zeros, product_zeros]
+    zeros = [within_zeros + factor_zeros, product_zeros]
     before_shard = jnp.zeros(back.shape, F32)
     for bit in bits:
         other = swapped(packed, "seq", bit)

time: 49.6 us -> 48 us (0.968)
  waiting for transfers between devices: 9.29 us -> 6.4 us
  starting transfers between devices: 15.2 us -> 16.8 us
    ppermute x5, waiting for transfers between devices: 8.99 us -> 5.39 us  [shifted(): lax.ppermute(value, axis, [(source, source + steps) for source in range(f...]
    ppermute x3, starting transfers between devices: 5.03 us -> 6.65 us  [swapped(): lax.ppermute(value, axis, [(source, source ^ bit) for source in range(cou...]
    ppermute x3, waiting for transfers between devices: 0.3 us -> 1.02 us  [swapped(): lax.ppermute(value, axis, [(source, source ^ bit) for source in range(cou...]
    pallas_call x2 -> x3, Pallas kernels: 6.77 us -> 6.41 us  [the longest x1 3.27 us: per_device(): call(product_kernel, 'product', [twice(spec) for spec in (wide, wide, tab...]
  transfers between devices with their start and end apart: 8 -> 8, of which waited for: 4 -> 4; matrix products, arithmetic and copies ran while one was open for 0% -> 0% of each run, Pallas kernels for 40% -> 41%
where the time goes in v2:
time: 48 us; the launch traced here: 47.7 us
  Pallas kernels  23.4 us (49%)
  starting transfers between devices  16.8 us (35%)
  waiting for transfers between devices  6.4 us (13%)
  between operations  0.9 us (2%)
    ppermute x5, starting transfers between devices, shifted(): lax.ppermute(value, axis, [(source, source + steps) for source in range(f...  10.1 us
    ppermute x3, starting transfers between devices, swapped(): lax.ppermute(value, axis, [(source, source ^ bit) for source in range(cou...  6.65 us
    pallas_call x1, Pallas kernels, per_device(): call(forward_kernel, 'forward', [twice(spec) for spec in [wide, wide, tab...  6.35 us
    ppermute x5, waiting for transfers between devices, shifted(): lax.ppermute(value, axis, [(source, source + steps) for source in range(f...  5.39 us
    pallas_call x1, Pallas kernels, per_device(): call(product_kernel, 'product', [twice(spec) for spec in (wide, wide, tab...  3.27 us
    pallas_call x1, Pallas kernels, per_device(): call(within_kernel, 'within', [wide, table, wide, wide, wide, wide], [wid...  3.07 us
    pallas_call x1, Pallas kernels, per_device(): call(local_kernel, 'local', [wide, wide, table], [wide], [wide_full])  2.26 us
    pallas_call x1, Pallas kernels, per_device(): call(gate_kernel, 'gate', [distant] * 2, [distant], [wide_half], [pltpu.V...  2.15 us
  transfers between devices with their start and end apart: 8, of which 4 were waited for; matrix products, arithmetic and copies ran while one was open for 0% of the time, Pallas kernels for 41%

profile of v2, /device:TPU:0, one launch (start us, length us, event | category | flops | bytes accessed | tf_op | source)
XLA Modules:
  0.0 47.7 jit_solution(15440066171334681018)
XLA Ops:
  0.6 0.0 copy-start
  0.6 0.0 copy-start.3
  0.7 0.0 copy-start.8
  0.7 2.1 %gate.1.now = bf16[2048,128]{1,0:T(8,128)(2,1)} custom-call(bf16[2048,128]{1,0:T(8,128)(2,1)} %bitcast.27, bf16[2048,128]{1,0:T(8,128)(2,1)} %bitcast.29), custom_call_target="tpu_custom_call" | custom-call | bytes 1 | tf_op jit(solution)/shard_map/gate/pallas_call | solution.py:497
  2.8 5.0 %collective-permute-start.3 = (bf16[2048,128]{1,0:T(8,128)(2,1)}, bf16[2048,128]{1,0:T(8,128)(2,1)S(1)}, u32[]{:S(2)}, u32[]{:S(2)}) collective-permute-start(bf16[2048,128]{1,0:T(8,128)(2,1)} %gate.1.now), channel_id=1, source_target_pairs={{0,8},{8,16},{16,24},{1,9},{9,17},{17,25},{2,10},{10,18},{18,26},{... | collective-permute-start | bytes 1572872 | tf_op jit(solution)/shard_map/ppermute | solution.py:429
  7.8 0.0 copy-done
  7.8 0.0 copy-done.3
  7.8 0.0 copy-done.8
  7.8 0.0 copy-start.7
  7.8 0.0 copy-start.9
  7.8 1.2 %state.1 = bf16[16,16,128]{2,1,0:T(8,128)(2,1)S(1)} custom-call(bf16[2048,128]{1,0:T(8,128)(2,1)S(1)} %bitcast.14, bf16[2048,128]{1,0:T(8,128)(2,1)S(1)} %bitcast.24, f32[16,128]{1,0:T(8,128)S(1)} %bitcast.31), custom_call_target="tpu_custom_call" | custom-call | bytes 1 | tf_op jit(solution)/shard_map/state/pallas_call | solution.py:507
  9.0 1.3 %collective-permute-start.2 = (bf16[16,16,128]{2,1,0:T(8,128)(2,1)S(1)}, bf16[16,16,128]{2,1,0:T(8,128)(2,1)S(1)}, u32[]{:S(2)}, u32[]{:S(2)}) collective-permute-start(bf16[16,16,128]{2,1,0:T(8,128)(2,1)S(1)} %state.1), channel_id=1, source_target_pairs={{24,0},{25,1},{26,2},{27,3},{28,4},{29,5},{30,6},{31,7}} | collective-permute-start | bytes 196616 | tf_op jit(solution)/shard_map/ppermute | solution.py:429
  10.3 1.3 %collective-permute-start.1 = (bf16[16,16,128]{2,1,0:T(8,128)(2,1)S(1)}, bf16[16,16,128]{2,1,0:T(8,128)(2,1)S(1)}, u32[]{:S(2)}, u32[]{:S(2)}) collective-permute-start(bf16[16,16,128]{2,1,0:T(8,128)(2,1)S(1)} %state.1), channel_id=1, source_target_pairs={{16,0},{24,8},{17,1},{25,9},{18,2},{26,10},{19,3},{27,11},{20,4},{... | collective-permute-start | bytes 196616 | tf_op jit(solution)/shard_map/ppermute | solution.py:429
  11.6 1.3 %collective-permute-start = (bf16[16,16,128]{2,1,0:T(8,128)(2,1)S(1)}, bf16[16,16,128]{2,1,0:T(8,128)(2,1)S(1)}, u32[]{:S(2)}, u32[]{:S(2)}) collective-permute-start(bf16[16,16,128]{2,1,0:T(8,128)(2,1)S(1)} %state.1), channel_id=1, source_target_pairs={{8,0},{16,8},{24,16},{9,1},{17,9},{25,17},{10,2},{18,10},{26,18},{... | collective-permute-start | bytes 196616 | tf_op jit(solution)/shard_map/ppermute | solution.py:429
  12.9 0.0 copy-done.7
  12.9 0.0 copy-done.9
  12.9 1.6 %table.1 = (bf16[2048,128]{1,0:T(8,128)(2,1)S(1)}, bf16[2048,128]{1,0:T(8,128)(2,1)S(1)}, bf16[2048,128]{1,0:T(8,128)(2,1)S(1)}, bf16[2048,128]{1,0:T(8,128)(2,1...) custom-call(f32[16,128]{1,0:T(8,128)S(1)} %bitcast.32, ...), custom_call_target="tpu_custom_call" | custom-call | bytes 1 | tf_op jit(solution)/shard_map/table/pallas_call | solution.py:512
  14.5 0.0 copy-start.1
  14.5 0.0 copy-start.2
  14.5 2.3 %local.1 = f32[2048,128]{1,0:T(8,128)S(1)} custom-call(bf16[2048,128]{1,0:T(8,128)(2,1)S(1)} %bitcast.15, bf16[2048,128]{1,0:T(8,128)(2,1)S(1)} %bitcast.25, f32[128,128]{1,0:T(8,128)S(1)} %get-tuple-element.35.turned), custom_call_target="tpu_custom_call" | custom-call | bytes 1 | tf_op jit(solution)/shard_map/local/pallas_call | solution.py:522
  16.8 0.9 %collective-permute-done.2 = bf16[16,16,128]{2,1,0:T(8,128)(2,1)S(1)} collective-permute-done((bf16[16,16,128]{2,1,0:T(8,128)(2,1)S(1)}, bf16[16,16,128]{2,1,0:T(8,128)(2,1)S(1)}, u32[]{:S(2)}, u32[]{:S(2)}) %collective-permute-start.2) | collective-permute-done | bytes 65568 | tf_op jit(solution)/shard_map/ppermute | solution.py:429
  17.7 2.1 %collective-permute-done.1 = bf16[16,16,128]{2,1,0:T(8,128)(2,1)S(1)} collective-permute-done((bf16[16,16,128]{2,1,0:T(8,128)(2,1)S(1)}, bf16[16,16,128]{2,1,0:T(8,128)(2,1)S(1)}, u32[]{:S(2)}, u32[]{:S(2)}) %collective-permute-start.1) | collective-permute-done | bytes 65568 | tf_op jit(solution)/shard_map/ppermute | solution.py:429
  19.8 0.0 collective-permute-done
  19.8 0.1 exponential_multiply_fusion.states.after_shard
  19.8 0.0 collective-permute-done.3.before
  19.8 0.0 copy-done.1
  19.9 0.0 copy-done.2
  19.9 0.0 copy-start.4
  19.9 1.1 %middle.1 = (bf16[2048,128]{1,0:T(8,128)(2,1)S(1)}, f32[2048,128]{1,0:T(8,128)S(1)}) custom-call(f32[16,16,128]{2,1,0:T(8,128)S(1)} %exponential_multiply_fusion.states.after_shard, f32[2048,128]{1,0:T(8,128)S(1)} %local.1, bf16[2048,128]{1,0:T(8,128)(2,1)S(1)} %get-tuple-element.36.to_next, bf16[2048,128]{1,0:T(8,128)(2,1)S(1)} %bitcast.18, ...), custom_call_target="tpu_custom_call" | custom-call | bytes 1 | tf_op jit(solution)/shard_map/middle/pallas_call | solution.py:528
  21.0 1.3 %collective-permute-start.4 = (bf16[2048,128]{1,0:T(8,128)(2,1)S(1)}, bf16[2048,128]{1,0:T(8,128)(2,1)S(1)}, u32[]{:S(2)}, u32[]{:S(2)}) collective-permute-start(bf16[2048,128]{1,0:T(8,128)(2,1)S(1)} %get-tuple-element.37.dz1), channel_id=1, source_target_pairs={{8,0},{16,8},{24,16},{9,1},{17,9},{25,17},{10,2},{18,10},{26,18},{... | collective-permute-start | bytes 1572872 | tf_op jit(solution)/shard_map/ppermute | solution.py:429
  22.3 0.0 copy-done.4
  22.3 6.3 %forward.1 = (f32[2048,128]{1,0:T(8,128)S(1)}, bf16[2048,128]{1,0:T(8,128)(2,1)S(1)}, bf16[25,16,128]{2,1,0:T(8,128)(2,1)S(1)}) custom-call(bf16[2048,128]{1,0:T(8,128)(2,1)S(1)} %collective-permute-done.3.before, bf16[2048,128]{1,0:T(8,128)(2,1)S(1)} %copy-done.4, bf16[128,128]{1,0:T(8,128)(2,1)S(1)} %copy-done.7, bf16[2048,128]{1,0:T(8,128)(2,1)S(1)} %bitcast.22, ...), custom_call_target="tpu_custom_call" | custom-call | bytes 1 | tf_op jit(solution)/shard_map/forward/pallas_call | solution.py:536
  28.6 2.7 %collective-permute-start.5 = (bf16[25,16,128]{2,1,0:T(8,128)(2,1)S(1)}, bf16[25,16,128]{2,1,0:T(8,128)(2,1)S(1)}, u32[]{:S(2)}, u32[]{:S(2)}) collective-permute-start(bf16[25,16,128]{2,1,0:T(8,128)(2,1)S(1)} %get-tuple-element.50), channel_id=1, source_target_pairs={{0,8},{8,0},{16,24},{24,16},{1,9},{9,1},{17,25},{25,17},{2,10},{10... | collective-permute-start | bytes 307208 | tf_op jit(solution)/shard_map/ppermute | solution.py:434
  31.3 3.1 %within.1 = (f32[2048,128]{1,0:T(8,128)S(1)}, bf16[2048,128]{1,0:T(8,128)(2,1)}, bf16[2048,128]{1,0:T(8,128)(2,1)}, f32[9,16,128]{2,1,0:T(8,128)S(1)}) custom-call(bf16[2048,128]{1,0:T(8,128)(2,1)S(1)} %get-tuple-element.43.u2, f32[128,128]{1,0:T(8,128)S(1)} %get-tuple-element.44.taps, f32[2048,128]{1,0:T(8,128)S(1)} %get-tuple-element.45.z1, ...), custom_call_target="tpu_custom_call" | custom-call | bytes 1 | tf_op jit(solution)/shard_map/within/pallas_call | solution.py:550
  34.4 2.4 %collective-permute-done.4.later = bf16[2048,128]{1,0:T(8,128)(2,1)S(1)} collective-permute-done((bf16[2048,128]{1,0:T(8,128)(2,1)S(1)}, bf16[2048,128]{1,0:T(8,128)(2,1)S(1)}, u32[]{:S(2)}, u32[]{:S(2)}) %collective-permute-start.4) | collective-permute-done | bytes 524320 | tf_op jit(solution)/shard_map/ppermute | solution.py:429
  36.8 0.0 copy-start.6
  36.8 0.1 factor.1
  36.8 0.0 copy-start.5
  36.9 1.0 %collective-permute-done.5 = bf16[25,16,128]{2,1,0:T(8,128)(2,1)S(1)} collective-permute-done((bf16[25,16,128]{2,1,0:T(8,128)(2,1)S(1)}, bf16[25,16,128]{2,1,0:T(8,128)(2,1)S(1)}, u32[]{:S(2)}, u32[]{:S(2)}) %collective-permute-start.5) | collective-permute-done | bytes 102432 | tf_op jit(solution)/shard_map/ppermute | solution.py:434
  37.9 3.9 %collective-permute-start.6 = (bf16[25,16,128]{2,1,0:T(8,128)(2,1)S(1)}, bf16[25,16,128]{2,1,0:T(8,128)(2,1)S(1)}, u32[]{:S(2)}, u32[]{:S(2)}) collective-permute-start(bf16[25,16,128]{2,1,0:T(8,128)(2,1)S(1)} %pad_maximum_fusion), channel_id=1, source_target_pairs={{0,16},{8,24},{16,0},{24,8},{1,17},{9,25},{17,1},{25,9},{2,18},{10... | collective-permute-start | bytes 307208 | tf_op jit(solution)/shard_map/ppermute | solution.py:434
  41.9 0.0 copy-done.6
  41.9 0.0 copy-done.5
  41.9 3.3 %product.1 = (bf16[2048,128]{1,0:T(8,128)(2,1)}, bf16[2048,128]{1,0:T(8,128)(2,1)}, f32[9,16,128]{2,1,0:T(8,128)S(1)}) custom-call(bf16[2048,128]{1,0:T(8,128)(2,1)S(1)} %get-tuple-element.37.dz1, bf16[2048,128]{1,0:T(8,128)(2,1)S(1)} %collective-permute-done.4.later, f32[128,128]{1,0:T(8,128)S(1)} %get-tuple-element.38.turned, ...), custom_call_target="tpu_custom_call" | custom-call | bytes 1 | tf_op jit(solution)/shard_map/product/pallas_call | solution.py:562
  45.1 0.0 collective-permute-done.6
  45.2 0.1 collective-permute-start.7
  45.3 1.8 %value.1 = bf16[2048,128]{1,0:T(8,128)(2,1)} custom-call(f32[16,16,128]{2,1,0:T(8,128)S(1)} %fusion.states, bf16[2048,128]{1,0:T(8,128)(2,1)S(1)} %get-tuple-element.56.after, f32[2048,128]{1,0:T(8,128)S(1)} %get-tuple-element.57.z2, bf16[2048,128]{1,0:T(8,128)(2,1)S(1)} %bitcast.17), custom_call_target="tpu_custom_call" | custom-call | bytes 1 | tf_op jit(solution)/shard_map/value/pallas_call | solution.py:585
  47.0 0.0 collective-permute-done.7.other
  47.1 0.6 %last.1 = (f32[128,128]{1,0:T(8,128)}, f32[16,128]{1,0:T(8,128)}) custom-call(bf16[9,16,128]{2,1,0:T(8,128)(2,1)S(1)} %add_convert_fusion.half, bf16[9,16,128]{2,1,0:T(8,128)(2,1)S(1)} %collective-permute-done.7.other), custom_call_target="tpu_custom_call" | custom-call | bytes 1 | tf_op jit(solution)/shard_map/last/pallas_call | solution.py:591
  (5 shorter events, 0.1 us)
Async XLA Ops:
  0.6 7.2 %copy-start = (bf16[1,2048,128]{2,1,0:T(8,128)(2,1)S(1)}, bf16[1,2048,128]{2,1,0:T(8,128)(2,1)}, u32[]{:S(2)}) copy-start(bf16[1,2048,128]{2,1,0:T(8,128)(2,1)} %param.14) | copy-start | bytes 1572868
  0.6 7.2 %copy-start.3 = (bf16[1,2048,128]{2,1,0:T(8,128)(2,1)S(1)}, bf16[1,2048,128]{2,1,0:T(8,128)(2,1)}, u32[]{:S(2)}) copy-start(bf16[1,2048,128]{2,1,0:T(8,128)(2,1)} %param.13) | copy-start | bytes 1572868
  0.7 7.2 %copy-start.8 = (f32[128,16]{0,1:T(8,128)S(1)}, f32[128,16]{0,1:T(8,128)}, u32[]{:S(2)}) copy-start(f32[128,16]{0,1:T(8,128)} %param.17) | copy-start | bytes 24580
  2.8 17.0 %collective-permute-start.3 = (bf16[2048,128]{1,0:T(8,128)(2,1)}, bf16[2048,128]{1,0:T(8,128)(2,1)S(1)}, u32[]{:S(2)}, u32[]{:S(2)}) collective-permute-start(bf16[2048,128]{1,0:T(8,128)(2,1)} %gate.1.now), channel_id=1, source_target_pairs={{0,8},{8,16},{16,24},{1,9},{9,17},{17,25},{2,10},{10,18},{18,26},{... | collective-permute-start | bytes 1572872 | tf_op jit(solution)/shard_map/ppermute | solution.py:429
  7.8 5.1 %copy-start.7 = (bf16[128,128]{1,0:T(8,128)(2,1)S(1)}, bf16[128,128]{1,0:T(8,128)(2,1)}, u32[]{:S(2)}) copy-start(bf16[128,128]{1,0:T(8,128)(2,1)} %filters.3) | copy-start | bytes 98308
  7.8 5.1 %copy-start.9 = (f32[128,16]{0,1:T(8,128)S(1)}, f32[128,16]{0,1:T(8,128)}, u32[]{:S(2)}) copy-start(f32[128,16]{0,1:T(8,128)} %param.16) | copy-start | bytes 24580
  9.0 8.7 %collective-permute-start.2 = (bf16[16,16,128]{2,1,0:T(8,128)(2,1)S(1)}, bf16[16,16,128]{2,1,0:T(8,128)(2,1)S(1)}, u32[]{:S(2)}, u32[]{:S(2)}) collective-permute-start(bf16[16,16,128]{2,1,0:T(8,128)(2,1)S(1)} %state.1), channel_id=1, source_target_pairs={{24,0},{25,1},{26,2},{27,3},{28,4},{29,5},{30,6},{31,7}} | collective-permute-start | bytes 196616 | tf_op jit(solution)/shard_map/ppermute | solution.py:429
  10.3 9.4 %collective-permute-start.1 = (bf16[16,16,128]{2,1,0:T(8,128)(2,1)S(1)}, bf16[16,16,128]{2,1,0:T(8,128)(2,1)S(1)}, u32[]{:S(2)}, u32[]{:S(2)}) collective-permute-start(bf16[16,16,128]{2,1,0:T(8,128)(2,1)S(1)} %state.1), channel_id=1, source_target_pairs={{16,0},{24,8},{17,1},{25,9},{18,2},{26,10},{19,3},{27,11},{20,4},{... | collective-permute-start | bytes 196616 | tf_op jit(solution)/shard_map/ppermute | solution.py:429
  11.6 8.2 %collective-permute-start = (bf16[16,16,128]{2,1,0:T(8,128)(2,1)S(1)}, bf16[16,16,128]{2,1,0:T(8,128)(2,1)S(1)}, u32[]{:S(2)}, u32[]{:S(2)}) collective-permute-start(bf16[16,16,128]{2,1,0:T(8,128)(2,1)S(1)} %state.1), channel_id=1, source_target_pairs={{8,0},{16,8},{24,16},{9,1},{17,9},{25,17},{10,2},{18,10},{26,18},{... | collective-permute-start | bytes 196616 | tf_op jit(solution)/shard_map/ppermute | solution.py:429
  14.5 5.4 %copy-start.1 = (bf16[1,2048,128]{2,1,0:T(8,128)(2,1)S(1)}, bf16[1,2048,128]{2,1,0:T(8,128)(2,1)}, u32[]{:S(2)}) copy-start(bf16[1,2048,128]{2,1,0:T(8,128)(2,1)} %param.12) | copy-start | bytes 1572868
  14.5 5.4 %copy-start.2 = (bf16[1,2048,128]{2,1,0:T(8,128)(2,1)S(1)}, bf16[1,2048,128]{2,1,0:T(8,128)(2,1)}, u32[]{:S(2)}) copy-start(bf16[1,2048,128]{2,1,0:T(8,128)(2,1)} %param.11) | copy-start | bytes 1572868
  19.9 2.4 %copy-start.4 = (bf16[2048,128]{1,0:T(8,128)(2,1)S(1)}, bf16[2048,128]{1,0:T(8,128)(2,1)}, u32[]{:S(2)}) copy-start(bf16[2048,128]{1,0:T(8,128)(2,1)} %gate.1.now) | copy-start | bytes 1572868
  21.0 15.8 %collective-permute-start.4 = (bf16[2048,128]{1,0:T(8,128)(2,1)S(1)}, bf16[2048,128]{1,0:T(8,128)(2,1)S(1)}, u32[]{:S(2)}, u32[]{:S(2)}) collective-permute-start(bf16[2048,128]{1,0:T(8,128)(2,1)S(1)} %get-tuple-element.37.dz1), channel_id=1, source_target_pairs={{8,0},{16,8},{24,16},{9,1},{17,9},{25,17},{10,2},{18,10},{26,18},{... | collective-permute-start | bytes 1572872 | tf_op jit(solution)/shard_map/ppermute | solution.py:429
  28.6 9.2 %collective-permute-start.5 = (bf16[25,16,128]{2,1,0:T(8,128)(2,1)S(1)}, bf16[25,16,128]{2,1,0:T(8,128)(2,1)S(1)}, u32[]{:S(2)}, u32[]{:S(2)}) collective-permute-start(bf16[25,16,128]{2,1,0:T(8,128)(2,1)S(1)} %get-tuple-element.50), channel_id=1, source_target_pairs={{0,8},{8,0},{16,24},{24,16},{1,9},{9,1},{17,25},{25,17},{2,10},{10... | collective-permute-start | bytes 307208 | tf_op jit(solution)/shard_map/ppermute | solution.py:434
  36.8 5.1 %copy-start.6 = (bf16[1,2048,128]{2,1,0:T(8,128)(2,1)S(1)}, bf16[1,2048,128]{2,1,0:T(8,128)(2,1)}, u32[]{:S(2)}) copy-start(bf16[1,2048,128]{2,1,0:T(8,128)(2,1)} %param.10) | copy-start | bytes 1572868
  36.8 5.0 %copy-start.5 = (bf16[1,2048,128]{2,1,0:T(8,128)(2,1)S(1)}, bf16[1,2048,128]{2,1,0:T(8,128)(2,1)}, u32[]{:S(2)}) copy-start(bf16[1,2048,128]{2,1,0:T(8,128)(2,1)} %param.9) | copy-start | bytes 1572868
  37.9 7.2 %collective-permute-start.6 = (bf16[25,16,128]{2,1,0:T(8,128)(2,1)S(1)}, bf16[25,16,128]{2,1,0:T(8,128)(2,1)S(1)}, u32[]{:S(2)}, u32[]{:S(2)}) collective-permute-start(bf16[25,16,128]{2,1,0:T(8,128)(2,1)S(1)} %pad_maximum_fusion), channel_id=1, source_target_pairs={{0,16},{8,24},{16,0},{24,8},{1,17},{9,25},{17,1},{25,9},{2,18},{10... | collective-permute-start | bytes 307208 | tf_op jit(solution)/shard_map/ppermute | solution.py:434
  45.2 1.9 %collective-permute-start.7 = (bf16[9,16,128]{2,1,0:T(8,128)(2,1)S(1)}, bf16[9,16,128]{2,1,0:T(8,128)(2,1)S(1)}, u32[]{:S(2)}, u32[]{:S(2)}) collective-permute-start(bf16[9,16,128]{2,1,0:T(8,128)(2,1)S(1)} %add_convert_fusion.half), channel_id=1, source_target_pairs={{0,1},{1,0},{2,3},{3,2},{4,5},{5,4},{6,7},{7,6},{8,9},{9,8},{10,11... | collective-permute-start | bytes 110600 | tf_op jit(solution)/shard_map/ppermute | solution.py:434

commit v3 on v2

--- a/solution.py
+++ b/solution.py
@@ -14,6 +14,7 @@
 PACK = TILE // LANES
 CHUNK = 32
 STEPS = 4
+PIECES = 8
 VMEM_LIMIT = 24 * 1024 * 1024
 
 
@@ -160,7 +161,7 @@
 
 
 def gate_kernel(query, key, product, held, made, arrived, left):
-    size = held.shape[1] // STEPS
+    size = held.shape[1] // PIECES
 
     def fetch(array, step):
         span = pl.ds(step * size, size)
@@ -172,16 +173,16 @@
         span = pl.ds(step * size, size)
         return pltpu.make_async_copy(made.at[span, :], product.at[span, :], left.at[step])
 
-    for step in range(STEPS):
+    for step in range(PIECES):
         for array in range(2):
             fetch(array, step).start()
-    for step in range(STEPS):
+    for step in range(PIECES):
         for array in range(2):
             fetch(array, step).wait()
         span = pl.ds(step * size, size)
         made[span, :] = held[0, span, :] * held[1, span, :]
         store(step).start()
-    for step in range(STEPS):
+    for step in range(PIECES):
         store(step).wait()
 
 
@@ -199,8 +200,8 @@
         state[block] = squeeze_groups(nt(powers, dz2), mask).astype(BF16)
 
 
-def table_kernel(
-    rate, residue, filters, to_next, after, to_end, power, taps, turned, mr_turned, wide_rate
+def local_kernel(
+    grad, value, rate, residue, filters, du2, to_next, after, to_end, power, taps, mr_turned, wide_rate
 ):
     rows, cols = iotas()
     mask = rows // LANES == cols // LANES
@@ -225,31 +226,29 @@
         to_next[span, :] = (ends * scale).astype(BF16)
         sums.append(jnp.sum(scaled.reshape(PACK, LANES, TILE), axis=1))
     taps[...] = above(*sums)
-    turned[...] = nn(above(*sums).astype(BF16), reversal())
+    turned = nn(above(*sums).astype(BF16), reversal())
     mr_turned[...] = nn(filters[...], reversal())
-
-
-def spans(array):
-    return [pl.ds(block * TILE, TILE) for block in range(array.shape[0] // TILE)]
-
-
-def group_rows(table, block):
-    return table[pl.ds(block * PACK, PACK), :]
-
-
-def local_kernel(grad, value, turned, du2):
-    rows, cols = iotas()
     lower = ones_where(rows >= cols)
     lower_half = beside(lower, lower)
     results = [
-        within_shard(grad[span, :] * value[span, :], group_rows(turned, block), lower_half)
+        within_shard(
+            grad[span, :] * value[span, :], turned[block * PACK : (block + 1) * PACK], lower_half
+        )
         for block, span in enumerate(spans(grad))
     ]
     for span, result in zip(spans(grad), results):
         du2[span, :] = result
 
 
-def middle_kernel(states, local, to_next, li_key, value, before, dz1, du2):
+def spans(array):
+    return [pl.ds(block * TILE, TILE) for block in range(array.shape[0] // TILE)]
+
+
+def group_rows(table, block):
+    return table[pl.ds(block * PACK, PACK), :]
+
+
+def middle_kernel(states, local, to_next, li_key, value, dz1, du2):
     rows, cols = iotas()
     mask = rows // LANES == cols // LANES
     wides = [spread_groups(states[block], mask).T.astype(BF16) for block in range(states.shape[0])]
@@ -377,15 +376,7 @@
         grad_value[span, :] = (du2_here * li_key[span, :].astype(F32) * z1_here).astype(BF16)
 
 
-def last_kernel(half, other, grad_filter, grad_residue):
-    chunks = half.shape[0] - 1
-    for chunk in range(chunks):
-        grad_filter[pl.ds(chunk * LANES, LANES), :] = half[chunk].astype(F32) + other[chunk].astype(F32)
-    grad_residue[...] = half[chunks].astype(F32) + other[chunks].astype(F32)
-
-
-def product_kernel(dz1, later, turned, query, key, grad_query, grad_key, nothing):
-    nothing[...] = jnp.zeros_like(nothing)
+def product_kernel(dz1, later, turned, query, key, grad_query, grad_key):
     rows, cols = iotas()
     lower = ones_where(rows >= cols)
     lower_half = beside(lower, lower)
@@ -400,7 +391,14 @@
         grad_key[span, :] = (du1 * query[span, :].astype(F32)).astype(BF16)
 
 
-def value_kernel(states, after, z2, grad, grad_value, made, left):
+def value_kernel(
+    states, after, z2, grad, half, other, grad_value, grad_filter, grad_residue, made, left
+):
+    chunks = half.shape[0] - 1
+    for chunk in range(chunks):
+        both = half[chunk].astype(F32) + other[chunk].astype(F32)
+        grad_filter[pl.ds(chunk * LANES, LANES), :] = both
+    grad_residue[...] = half[chunks].astype(F32) + other[chunks].astype(F32)
     rows, cols = iotas()
     mask = rows // LANES == cols // LANES
     at = pl.program_id(0)
@@ -498,7 +496,7 @@
         gate_kernel, "gate", [distant] * 2, [distant], [wide_half],
         [
             pltpu.VMEM((2, channels, TILE), BF16), pltpu.VMEM((channels, TILE), BF16),
-            pltpu.SemaphoreType.DMA((2, STEPS)), pltpu.SemaphoreType.DMA((STEPS,)),
+            pltpu.SemaphoreType.DMA((2, PIECES)), pltpu.SemaphoreType.DMA((PIECES,)),
         ],
         grid=1, limit=60 * 1024 * 1024,
     )(query, key)
@@ -509,26 +507,22 @@
     )
 
     later_backs = [shifted(back, "seq", -gap) for gap in range(1, lax.axis_size("seq"))]
-    to_next, after, to_end, power, taps, turned, mr_turned, wide_rate = call(
-        table_kernel, "table", [modes, modes, table], [wide] * 4 + [table] * 3 + [chunk],
-        [wide_half] * 4 + [table_full] * 3 + [chunk_full],
-    )(rate, residue, mr_filter)
+    du2_local, to_next, after, to_end, power, taps, mr_turned, wide_rate = call(
+        local_kernel, "local",
+        [twice(wide), twice(wide), modes, modes, twice(table)],
+        [twice(wide)] * 5 + [twice(table)] * 2 + [twice(chunk)],
+        [wide_full] + [wide_half] * 4 + [table_full] * 2 + [chunk_full], grid=STEPS // 2,
+    )(grad, value_two, rate, residue, mr_filter)
     fade = jnp.exp(-TILE * wide_rate)
     after_shard = later_backs[-1].astype(F32)
     for other in later_backs[-2::-1]:
         after_shard = other.astype(F32) + fade * after_shard
     after_shard = after_shard * jnp.exp(-wide_rate)
 
-    (du2_local,) = call(
-        local_kernel, "local", [wide, wide, table], [wide], [wide_full]
-    )(
-        grad, value_two, turned
-    )
-
     dz1, du2 = call(
-        middle_kernel, "middle", [chunk, wide, wide, wide, wide, anywhere], [wide, wide],
-        [wide_half, wide_full],
-    )(after_shard, du2_local, to_next, key_two, value, product_before)
+        middle_kernel, "middle", [twice(chunk)] + [twice(wide)] * 4, [twice(wide)] * 2,
+        [wide_half, wide_full], grid=STEPS // 2,
+    )(after_shard, du2_local, to_next, key_two, value)
     dz1_later = shifted(dz1, "seq", -1)
 
     filter_chunks = groups // LANES
@@ -559,39 +553,38 @@
         grid=1,
     )(wide_rate, dz1_later)
 
-    grad_query, grad_key, product_zeros = call(
+    grad_query, grad_key = call(
         product_kernel, "product",
         [twice(spec) for spec in (wide, wide, table, wide, wide)],
-        [twice(wide), twice(wide), whole(few_full)], [wide_half, wide_half, few_full],
-        grid=STEPS // 2,
+        [twice(wide), twice(wide)], [wide_half, wide_half], grid=STEPS // 2,
     )(dz1, dz1_later, mr_turned, query, key)
 
-    zeros = [within_zeros + factor_zeros, product_zeros]
+    assert lax.axis_size("dp") == 2
+    half = packed[blocks:]
+    sums = half.astype(F32) + swapped(half, "dp", 1).astype(F32) + within_zeros
+    packed = jnp.concatenate([packed[:blocks], sums.astype(BF16)], axis=0)
+    zeros = [factor_zeros]
     before_shard = jnp.zeros(back.shape, F32)
     for bit in bits:
         other = swapped(packed, "seq", bit)
-        sums = packed[blocks:].astype(F32) + other[blocks:].astype(F32)
-        if zeros:
-            sums = sums + zeros.pop(0)
         mine, theirs = packed[:blocks].astype(F32), other[:blocks].astype(F32)
         before_shard = before_shard + weights.pop(0) * theirs
+        half, partner = packed[blocks:], other[blocks:]
         if bit != bits[-1]:
+            sums = half.astype(F32) + partner.astype(F32)
+            if zeros:
+                sums = sums + zeros.pop(0)
             total = weights.pop(0) * theirs + weights.pop(0) * mine
             packed = jnp.concatenate([total.astype(BF16), sums.astype(BF16)], axis=0)
-    sums = sums.astype(BF16)
-
-    assert lax.axis_size("dp") == 2
-    partner = swapped(sums, "dp", 1)
-    (grad_li_value,) = call(
-        value_kernel, "value", [chunk, wide, wide, wide], [distant], [wide_half],
+    residue_full = jax.ShapeDtypeStruct((LANES, TILE), F32)
+    grad_li_value, grad_filter, grad_residue = call(
+        value_kernel, "value",
+        [chunk, wide, wide, wide, whole(half), whole(half)],
+        [distant, whole(table_full), whole(residue_full)],
+        [wide_half, table_full, residue_full],
         [pltpu.VMEM((channels, TILE), BF16), pltpu.SemaphoreType.DMA((STEPS,))],
-    )(before_shard, after, z2, grad)
-
-    residue_full = jax.ShapeDtypeStruct((LANES, TILE), F32)
-    grad_filter, grad_residue = call(
-        last_kernel, "last", [whole(sums)] * 2,
-        [whole(table_full), whole(residue_full)], [table_full, residue_full], grid=1,
-    )(sums, partner)
+    )(before_shard, after, z2, grad, half, partner)
+
     return (
         grad_query[None],
         grad_key[None],

time: 48 us -> 48.3 us (level)
  waiting for transfers between devices: 6.4 us -> 8 us
  starting transfers between devices: 16.8 us -> 15.4 us
    ppermute x3, waiting for transfers between devices: 1.02 us -> 4.48 us  [swapped(): lax.ppermute(value, axis, [(source, source ^ bit) for source in range(cou...]
    ppermute x5, waiting for transfers between devices: 5.39 us -> 3.52 us  [shifted(): lax.ppermute(value, axis, [(source, source + steps) for source in range(f...]
    ppermute x3, starting transfers between devices: 6.65 us -> 5.28 us  [swapped(): lax.ppermute(value, axis, [(source, source ^ bit) for source in range(cou...]
    pallas_call x5 -> x3, Pallas kernels: 7.32 us -> 7.37 us  [the longest x1 4.31 us: per_device(): call(local_kernel, 'local', [twice(wide), twice(wide), modes, modes, twic...]
  transfers between devices with their start and end apart: 8 -> 8, of which waited for: 4 -> 5; matrix products, arithmetic and copies ran while one was open for 0% -> 0% of each run, Pallas kernels for 41% -> 39%
where the time goes in v3:
time: 48.3 us; the launch traced here: 48.1 us
  Pallas kernels  23.5 us (49%)
  starting transfers between devices  15.4 us (32%)
  waiting for transfers between devices  8 us (17%)
  between operations  0.93 us (2%)
    ppermute x5, starting transfers between devices, shifted(): lax.ppermute(value, axis, [(source, source + steps) for source in range(f...  10.1 us
    pallas_call x1, Pallas kernels, per_device(): call(forward_kernel, 'forward', [twice(spec) for spec in [wide, wide, tab...  6.34 us
    ppermute x3, starting transfers between devices, swapped(): lax.ppermute(value, axis, [(source, source ^ bit) for source in range(cou...  5.28 us
    ppermute x3, waiting for transfers between devices, swapped(): lax.ppermute(value, axis, [(source, source ^ bit) for source in range(cou...  4.48 us
    pallas_call x1, Pallas kernels, per_device(): call(local_kernel, 'local', [twice(wide), twice(wide), modes, modes, twic...  4.31 us
    ppermute x5, waiting for transfers between devices, shifted(): lax.ppermute(value, axis, [(source, source + steps) for source in range(f...  3.52 us
    pallas_call x1, Pallas kernels, per_device(): call(product_kernel, 'product', [twice(spec) for spec in (wide, wide, tab...  3.27 us
    pallas_call x1, Pallas kernels, per_device(): call(within_kernel, 'within', [wide, table, wide, wide, wide, wide], [wid...  3.1 us
  transfers between devices with their start and end apart: 8, of which 5 were waited for; matrix products, arithmetic and copies ran while one was open for 0% of the time, Pallas kernels for 39%

profile of v3, /device:TPU:0, one launch (start us, length us, event | category | flops | bytes accessed | tf_op | source)
XLA Modules:
  0.0 48.1 jit_solution(503496212520134311)
XLA Ops:
  0.6 0.0 copy-start
  0.6 0.0 copy-start.1
  0.7 0.0 copy-start.8
  0.7 2.2 %gate.1.now = bf16[2048,128]{1,0:T(8,128)(2,1)} custom-call(bf16[2048,128]{1,0:T(8,128)(2,1)} %bitcast.27, bf16[2048,128]{1,0:T(8,128)(2,1)} %bitcast.29), custom_call_target="tpu_custom_call" | custom-call | bytes 1 | tf_op jit(solution)/shard_map/gate/pallas_call | solution.py:495
  2.8 5.0 %collective-permute-start.4 = (bf16[2048,128]{1,0:T(8,128)(2,1)}, bf16[2048,128]{1,0:T(8,128)(2,1)S(1)}, u32[]{:S(2)}, u32[]{:S(2)}) collective-permute-start(bf16[2048,128]{1,0:T(8,128)(2,1)} %gate.1.now), channel_id=1, source_target_pairs={{0,8},{8,16},{16,24},{1,9},{9,17},{17,25},{2,10},{10,18},{18,26},{... | collective-permute-start | bytes 1572872 | tf_op jit(solution)/shard_map/ppermute | solution.py:427
  7.8 0.0 copy-done
  7.8 0.0 copy-done.1
  7.8 0.0 copy-done.8
  7.8 0.0 copy-start.7
  7.8 0.0 copy-start.9
  7.9 1.2 %state.1 = bf16[16,16,128]{2,1,0:T(8,128)(2,1)S(1)} custom-call(bf16[2048,128]{1,0:T(8,128)(2,1)S(1)} %bitcast.14, bf16[2048,128]{1,0:T(8,128)(2,1)S(1)} %bitcast.18, f32[16,128]{1,0:T(8,128)S(1)} %bitcast.31), custom_call_target="tpu_custom_call" | custom-call | bytes 1 | tf_op jit(solution)/shard_map/state/pallas_call | solution.py:505
  9.0 1.3 %collective-permute-start.2 = (bf16[16,16,128]{2,1,0:T(8,128)(2,1)S(1)}, bf16[16,16,128]{2,1,0:T(8,128)(2,1)S(1)}, u32[]{:S(2)}, u32[]{:S(2)}) collective-permute-start(bf16[16,16,128]{2,1,0:T(8,128)(2,1)S(1)} %state.1), channel_id=1, source_target_pairs={{24,0},{25,1},{26,2},{27,3},{28,4},{29,5},{30,6},{31,7}} | collective-permute-start | bytes 196616 | tf_op jit(solution)/shard_map/ppermute | solution.py:427
  10.3 1.3 %collective-permute-start.1 = (bf16[16,16,128]{2,1,0:T(8,128)(2,1)S(1)}, bf16[16,16,128]{2,1,0:T(8,128)(2,1)S(1)}, u32[]{:S(2)}, u32[]{:S(2)}) collective-permute-start(bf16[16,16,128]{2,1,0:T(8,128)(2,1)S(1)} %state.1), channel_id=1, source_target_pairs={{16,0},{24,8},{17,1},{25,9},{18,2},{26,10},{19,3},{27,11},{20,4},{... | collective-permute-start | bytes 196616 | tf_op jit(solution)/shard_map/ppermute | solution.py:427
  11.6 1.3 %collective-permute-start = (bf16[16,16,128]{2,1,0:T(8,128)(2,1)S(1)}, bf16[16,16,128]{2,1,0:T(8,128)(2,1)S(1)}, u32[]{:S(2)}, u32[]{:S(2)}) collective-permute-start(bf16[16,16,128]{2,1,0:T(8,128)(2,1)S(1)} %state.1), channel_id=1, source_target_pairs={{8,0},{16,8},{24,16},{9,1},{17,9},{25,17},{10,2},{18,10},{26,18},{... | collective-permute-start | bytes 196616 | tf_op jit(solution)/shard_map/ppermute | solution.py:427
  12.9 0.0 copy-done.7
  12.9 0.0 copy-done.9
  12.9 0.0 copy-start.2
  13.0 0.0 copy-start.3
  13.0 4.3 %local.1 = (f32[2048,128]{1,0:T(8,128)S(1)}, bf16[2048,128]{1,0:T(8,128)(2,1)S(1)}, bf16[2048,128]{1,0:T(8,128)(2,1)S(1)}, bf16[2048,128]{1,0:T(8,128)(2,1)S(1)}...) custom-call(bf16[2048,128]{1,0:T(8,128)(2,1)S(1)} %bitcast.15, ...), custom_call_target="tpu_custom_call" | custom-call | bytes 1 | tf_op jit(solution)/shard_map/local/pallas_call | solution.py:510
  17.3 0.4 collective-permute-done.2
  17.7 2.1 %collective-permute-done.1 = bf16[16,16,128]{2,1,0:T(8,128)(2,1)S(1)} collective-permute-done((bf16[16,16,128]{2,1,0:T(8,128)(2,1)S(1)}, bf16[16,16,128]{2,1,0:T(8,128)(2,1)S(1)}, u32[]{:S(2)}, u32[]{:S(2)}) %collective-permute-start.1) | collective-permute-done | bytes 65568 | tf_op jit(solution)/shard_map/ppermute | solution.py:427
  19.8 0.0 collective-permute-done
  19.8 0.1 exponential_multiply_fusion.states.after_shard
  19.9 0.0 copy-done.2
  19.9 0.0 copy-done.3
  19.9 0.0 copy-start.4
  19.9 0.7 %middle.1 = (bf16[2048,128]{1,0:T(8,128)(2,1)S(1)}, f32[2048,128]{1,0:T(8,128)S(1)}) custom-call(f32[16,16,128]{2,1,0:T(8,128)S(1)} %exponential_multiply_fusion.states.after_shard, f32[2048,128]{1,0:T(8,128)S(1)} %get-tuple-element.35.local, bf16[2048,128]{1,0:T(8,128)(2,1)S(1)} %get-tuple-element.36.to_next, bf16[2048,128]{1,0:T(8,128)(2,1)S(1)} %bitcast.21, ...), custom_call_target="tpu_custom_call" | custom-call | bytes 1 | tf_op jit(solution)/shard_map/middle/pallas_call | solution.py:522
  20.6 1.3 %collective-permute-start.3 = (bf16[2048,128]{1,0:T(8,128)(2,1)S(1)}, bf16[2048,128]{1,0:T(8,128)(2,1)S(1)}, u32[]{:S(2)}, u32[]{:S(2)}) collective-permute-start(bf16[2048,128]{1,0:T(8,128)(2,1)S(1)} %get-tuple-element.37.dz1), channel_id=1, source_target_pairs={{8,0},{16,8},{24,16},{9,1},{17,9},{25,17},{10,2},{18,10},{26,18},{... | collective-permute-start | bytes 1572872 | tf_op jit(solution)/shard_map/ppermute | solution.py:427
  21.9 0.0 collective-permute-done.4.before
  21.9 0.0 copy-done.4
  21.9 6.3 %forward.1 = (f32[2048,128]{1,0:T(8,128)S(1)}, bf16[2048,128]{1,0:T(8,128)(2,1)S(1)}, bf16[25,16,128]{2,1,0:T(8,128)(2,1)S(1)}) custom-call(bf16[2048,128]{1,0:T(8,128)(2,1)S(1)} %collective-permute-done.4.before, bf16[2048,128]{1,0:T(8,128)(2,1)S(1)} %copy-done.4, bf16[128,128]{1,0:T(8,128)(2,1)S(1)} %copy-done.7, bf16[2048,128]{1,0:T(8,128)(2,1)S(1)} %bitcast.25, ...), custom_call_target="tpu_custom_call" | custom-call | bytes 1 | tf_op jit(solution)/shard_map/forward/pallas_call | solution.py:530
  28.2 0.1 collective-permute-start.5
  28.3 3.1 %within.1 = (f32[2048,128]{1,0:T(8,128)S(1)}, bf16[2048,128]{1,0:T(8,128)(2,1)}, bf16[2048,128]{1,0:T(8,128)(2,1)}, f32[9,16,128]{2,1,0:T(8,128)S(1)}) custom-call(bf16[2048,128]{1,0:T(8,128)(2,1)S(1)} %get-tuple-element.43.u2, f32[128,128]{1,0:T(8,128)S(1)} %get-tuple-element.44.taps, f32[2048,128]{1,0:T(8,128)S(1)} %get-tuple-element.45.z1, ...), custom_call_target="tpu_custom_call" | custom-call | bytes 1 | tf_op jit(solution)/shard_map/within/pallas_call | solution.py:544
  31.4 0.0 collective-permute-done.5
  31.5 2.7 %collective-permute-start.6 = (bf16[25,16,128]{2,1,0:T(8,128)(2,1)S(1)}, bf16[25,16,128]{2,1,0:T(8,128)(2,1)S(1)}, u32[]{:S(2)}, u32[]{:S(2)}) collective-permute-start(bf16[25,16,128]{2,1,0:T(8,128)(2,1)S(1)} %pad_maximum_fusion), channel_id=1, source_target_pairs={{0,8},{8,0},{16,24},{24,16},{1,9},{9,1},{17,25},{25,17},{2,10},{10... | collective-permute-start | bytes 307208 | tf_op jit(solution)/shard_map/ppermute | solution.py:432
  34.2 1.0 %collective-permute-done.3.later = bf16[2048,128]{1,0:T(8,128)(2,1)S(1)} collective-permute-done((bf16[2048,128]{1,0:T(8,128)(2,1)S(1)}, bf16[2048,128]{1,0:T(8,128)(2,1)S(1)}, u32[]{:S(2)}, u32[]{:S(2)}) %collective-permute-start.3) | collective-permute-done | bytes 524320 | tf_op jit(solution)/shard_map/ppermute | solution.py:427
  35.2 0.0 copy-start.6
  35.2 0.1 factor.1
  35.3 0.0 copy-start.5
  35.3 2.4 %collective-permute-done.6 = bf16[25,16,128]{2,1,0:T(8,128)(2,1)S(1)} collective-permute-done((bf16[25,16,128]{2,1,0:T(8,128)(2,1)S(1)}, bf16[25,16,128]{2,1,0:T(8,128)(2,1)S(1)}, u32[]{:S(2)}, u32[]{:S(2)}) %collective-permute-start.6) | collective-permute-done | bytes 102432 | tf_op jit(solution)/shard_map/ppermute | solution.py:432
  37.8 2.5 %collective-permute-start.7 = (bf16[25,16,128]{2,1,0:T(8,128)(2,1)S(1)}, bf16[25,16,128]{2,1,0:T(8,128)(2,1)S(1)}, u32[]{:S(2)}, u32[]{:S(2)}) collective-permute-start(bf16[25,16,128]{2,1,0:T(8,128)(2,1)S(1)} %pad_maximum_fusion.1), channel_id=1, source_target_pairs={{0,16},{8,24},{16,0},{24,8},{1,17},{9,25},{17,1},{25,9},{2,18},{10... | collective-permute-start | bytes 307208 | tf_op jit(solution)/shard_map/ppermute | solution.py:432
  40.3 0.0 copy-done.6
  40.3 0.0 copy-done.5
  40.3 3.3 %product.1 = (bf16[2048,128]{1,0:T(8,128)(2,1)}, bf16[2048,128]{1,0:T(8,128)(2,1)}) custom-call(bf16[2048,128]{1,0:T(8,128)(2,1)S(1)} %get-tuple-element.37.dz1, bf16[2048,128]{1,0:T(8,128)(2,1)S(1)} %collective-permute-done.3.later, f32[128,128]{1,0:T(8,128)S(1)} %get-tuple-element.38.turned, bf16[2048,128]{1,0:T(8,128)(2,1)S(1)} %bitcast.28, ...), custom_call_target="tpu_custom_call" | custom-call | bytes 1 | tf_op jit(solution)/shard_map/product/pallas_call | solution.py:556
  43.6 2.1 %collective-permute-done.7 = bf16[25,16,128]{2,1,0:T(8,128)(2,1)S(1)} collective-permute-done((bf16[25,16,128]{2,1,0:T(8,128)(2,1)S(1)}, bf16[25,16,128]{2,1,0:T(8,128)(2,1)S(1)}, u32[]{:S(2)}, u32[]{:S(2)}) %collective-permute-start.7) | collective-permute-done | bytes 102432 | tf_op jit(solution)/shard_map/ppermute | solution.py:432
  45.7 2.4 %value.1 = (bf16[2048,128]{1,0:T(8,128)(2,1)}, f32[128,128]{1,0:T(8,128)}, f32[16,128]{1,0:T(8,128)}) custom-call(f32[16,16,128]{2,1,0:T(8,128)S(1)} %fusion.states, bf16[2048,128]{1,0:T(8,128)(2,1)S(1)} %get-tuple-element.56.after, f32[2048,128]{1,0:T(8,128)S(1)} %get-tuple-element.57.z2, bf16[2048,128]{1,0:T(8,128)(2,1)S(1)} %bitcast.17, ...), custom_call_target="tpu_custom_call" | custom-call | bytes 1 | tf_op jit(solution)/shard_map/value/pallas_call | solution.py:580
  (9 shorter events, 0.2 us)
Async XLA Ops:
  0.6 7.2 %copy-start = (bf16[1,2048,128]{2,1,0:T(8,128)(2,1)S(1)}, bf16[1,2048,128]{2,1,0:T(8,128)(2,1)}, u32[]{:S(2)}) copy-start(bf16[1,2048,128]{2,1,0:T(8,128)(2,1)} %param.14) | copy-start | bytes 1572868
  0.6 7.2 %copy-start.1 = (bf16[1,2048,128]{2,1,0:T(8,128)(2,1)S(1)}, bf16[1,2048,128]{2,1,0:T(8,128)(2,1)}, u32[]{:S(2)}) copy-start(bf16[1,2048,128]{2,1,0:T(8,128)(2,1)} %param.13) | copy-start | bytes 1572868
  0.7 7.2 %copy-start.8 = (f32[128,16]{0,1:T(8,128)S(1)}, f32[128,16]{0,1:T(8,128)}, u32[]{:S(2)}) copy-start(f32[128,16]{0,1:T(8,128)} %param.17) | copy-start | bytes 24580
  2.8 19.0 %collective-permute-start.4 = (bf16[2048,128]{1,0:T(8,128)(2,1)}, bf16[2048,128]{1,0:T(8,128)(2,1)S(1)}, u32[]{:S(2)}, u32[]{:S(2)}) collective-permute-start(bf16[2048,128]{1,0:T(8,128)(2,1)} %gate.1.now), channel_id=1, source_target_pairs={{0,8},{8,16},{16,24},{1,9},{9,17},{17,25},{2,10},{10,18},{18,26},{... | collective-permute-start | bytes 1572872 | tf_op jit(solution)/shard_map/ppermute | solution.py:427
  7.8 5.1 %copy-start.7 = (bf16[128,128]{1,0:T(8,128)(2,1)S(1)}, bf16[128,128]{1,0:T(8,128)(2,1)}, u32[]{:S(2)}) copy-start(bf16[128,128]{1,0:T(8,128)(2,1)} %filters.3) | copy-start | bytes 98308
  7.8 5.1 %copy-start.9 = (f32[128,16]{0,1:T(8,128)S(1)}, f32[128,16]{0,1:T(8,128)}, u32[]{:S(2)}) copy-start(f32[128,16]{0,1:T(8,128)} %param.16) | copy-start | bytes 24580
  9.0 8.7 %collective-permute-start.2 = (bf16[16,16,128]{2,1,0:T(8,128)(2,1)S(1)}, bf16[16,16,128]{2,1,0:T(8,128)(2,1)S(1)}, u32[]{:S(2)}, u32[]{:S(2)}) collective-permute-start(bf16[16,16,128]{2,1,0:T(8,128)(2,1)S(1)} %state.1), channel_id=1, source_target_pairs={{24,0},{25,1},{26,2},{27,3},{28,4},{29,5},{30,6},{31,7}} | collective-permute-start | bytes 196616 | tf_op jit(solution)/shard_map/ppermute | solution.py:427
  10.3 9.4 %collective-permute-start.1 = (bf16[16,16,128]{2,1,0:T(8,128)(2,1)S(1)}, bf16[16,16,128]{2,1,0:T(8,128)(2,1)S(1)}, u32[]{:S(2)}, u32[]{:S(2)}) collective-permute-start(bf16[16,16,128]{2,1,0:T(8,128)(2,1)S(1)} %state.1), channel_id=1, source_target_pairs={{16,0},{24,8},{17,1},{25,9},{18,2},{26,10},{19,3},{27,11},{20,4},{... | collective-permute-start | bytes 196616 | tf_op jit(solution)/shard_map/ppermute | solution.py:427
  11.6 8.2 %collective-permute-start = (bf16[16,16,128]{2,1,0:T(8,128)(2,1)S(1)}, bf16[16,16,128]{2,1,0:T(8,128)(2,1)S(1)}, u32[]{:S(2)}, u32[]{:S(2)}) collective-permute-start(bf16[16,16,128]{2,1,0:T(8,128)(2,1)S(1)} %state.1), channel_id=1, source_target_pairs={{8,0},{16,8},{24,16},{9,1},{17,9},{25,17},{10,2},{18,10},{26,18},{... | collective-permute-start | bytes 196616 | tf_op jit(solution)/shard_map/ppermute | solution.py:427
  12.9 6.9 %copy-start.2 = (bf16[1,2048,128]{2,1,0:T(8,128)(2,1)S(1)}, bf16[1,2048,128]{2,1,0:T(8,128)(2,1)}, u32[]{:S(2)}) copy-start(bf16[1,2048,128]{2,1,0:T(8,128)(2,1)} %param.12) | copy-start | bytes 1572868
  13.0 6.9 %copy-start.3 = (bf16[1,2048,128]{2,1,0:T(8,128)(2,1)S(1)}, bf16[1,2048,128]{2,1,0:T(8,128)(2,1)}, u32[]{:S(2)}) copy-start(bf16[1,2048,128]{2,1,0:T(8,128)(2,1)} %param.11) | copy-start | bytes 1572868
  19.9 2.0 %copy-start.4 = (bf16[2048,128]{1,0:T(8,128)(2,1)S(1)}, bf16[2048,128]{1,0:T(8,128)(2,1)}, u32[]{:S(2)}) copy-start(bf16[2048,128]{1,0:T(8,128)(2,1)} %gate.1.now) | copy-start | bytes 1572868
  20.6 14.7 %collective-permute-start.3 = (bf16[2048,128]{1,0:T(8,128)(2,1)S(1)}, bf16[2048,128]{1,0:T(8,128)(2,1)S(1)}, u32[]{:S(2)}, u32[]{:S(2)}) collective-permute-start(bf16[2048,128]{1,0:T(8,128)(2,1)S(1)} %get-tuple-element.37.dz1), channel_id=1, source_target_pairs={{8,0},{16,8},{24,16},{9,1},{17,9},{25,17},{10,2},{18,10},{26,18},{... | collective-permute-start | bytes 1572872 | tf_op jit(solution)/shard_map/ppermute | solution.py:427
  28.2 3.2 %collective-permute-start.5 = (bf16[9,16,128]{2,1,0:T(8,128)(2,1)S(1)}, bf16[9,16,128]{2,1,0:T(8,128)(2,1)S(1)}, u32[]{:S(2)}, u32[]{:S(2)}) collective-permute-start(bf16[9,16,128]{2,1,0:T(8,128)(2,1)S(1)} %slice.19), channel_id=1, source_target_pairs={{0,1},{1,0},{2,3},{3,2},{4,5},{5,4},{6,7},{7,6},{8,9},{9,8},{10,11... | collective-permute-start | bytes 110600 | tf_op jit(solution)/shard_map/ppermute | solution.py:432
  31.5 6.2 %collective-permute-start.6 = (bf16[25,16,128]{2,1,0:T(8,128)(2,1)S(1)}, bf16[25,16,128]{2,1,0:T(8,128)(2,1)S(1)}, u32[]{:S(2)}, u32[]{:S(2)}) collective-permute-start(bf16[25,16,128]{2,1,0:T(8,128)(2,1)S(1)} %pad_maximum_fusion), channel_id=1, source_target_pairs={{0,8},{8,0},{16,24},{24,16},{1,9},{9,1},{17,25},{25,17},{2,10},{10... | collective-permute-start | bytes 307208 | tf_op jit(solution)/shard_map/ppermute | solution.py:432
  35.2 5.1 %copy-start.6 = (bf16[1,2048,128]{2,1,0:T(8,128)(2,1)S(1)}, bf16[1,2048,128]{2,1,0:T(8,128)(2,1)}, u32[]{:S(2)}) copy-start(bf16[1,2048,128]{2,1,0:T(8,128)(2,1)} %param.10) | copy-start | bytes 1572868
  35.3 5.0 %copy-start.5 = (bf16[1,2048,128]{2,1,0:T(8,128)(2,1)S(1)}, bf16[1,2048,128]{2,1,0:T(8,128)(2,1)}, u32[]{:S(2)}) copy-start(bf16[1,2048,128]{2,1,0:T(8,128)(2,1)} %param.9) | copy-start | bytes 1572868
  37.8 7.9 %collective-permute-start.7 = (bf16[25,16,128]{2,1,0:T(8,128)(2,1)S(1)}, bf16[25,16,128]{2,1,0:T(8,128)(2,1)S(1)}, u32[]{:S(2)}, u32[]{:S(2)}) collective-permute-start(bf16[25,16,128]{2,1,0:T(8,128)(2,1)S(1)} %pad_maximum_fusion.1), channel_id=1, source_target_pairs={{0,16},{8,24},{16,0},{24,8},{1,17},{9,25},{17,1},{25,9},{2,18},{10... | collective-permute-start | bytes 307208 | tf_op jit(solution)/shard_map/ppermute | solution.py:432
